TPU v7x, 128 devices: a whole 4x4x4 slice. The times are simulated.
128 devices in a mesh: fine: 4 (over y_lo, core), coarse: 32 (over x, y_hi, z).
Axes of the slice: x: 4, y: 4 (y_hi: 2, y_lo: 2; y = y_hi * 2 + y_lo), z: 4, core: 2. Of those that a mesh axis runs over, the one named last changes fastest.
Arguments:
- node_state: bfloat16 [131072, 128], P(('fine', 'coarse')), may hold values from -6 to 6
- fine_edge_state: bfloat16 [524288, 128], P(('fine', 'coarse')), may hold values from -6 to 6
- coarse_edge_state: bfloat16 [81920, 128], P(('fine', 'coarse')), may hold values from -6 to 6
- fine_src: int32 [524288], P(('fine', 'coarse')), may hold values from 0 to 1535
- fine_dst: int32 [524288], P(('fine', 'coarse')), may hold values from 0 to 1023
- halo_rows: int32 [512, 128], P(('fine', 'coarse')), may hold values from 0 to 1023
- block_owner: int32 [8192, 1], P(('fine', 'coarse')), may hold values from 0 to 31; in each aligned block of 64 rows (0 to 63, 64 to 127, ...) at most 5 rows name the same one
- coarse_src: int32 [81920], P(('fine', 'coarse')), may hold values from 0 to 479
- coarse_dst: int32 [81920], P(('fine', 'coarse')), may hold values from 0 to 159
- cotangent: bfloat16 [131072, 128], P(('fine', 'coarse')), may hold values from -6 to 6
- fine_edge_in: bfloat16 [2, 384, 128], replicated, may hold values from -0.3125 to 0.3125
- fine_edge_out: bfloat16 [2, 128, 128], replicated, may hold values from -0.5 to 0.5
- fine_node_in: bfloat16 [2, 256, 128], replicated, may hold values from -0.375 to 0.375
- fine_node_out: bfloat16 [2, 128, 128], replicated, may hold values from -0.5 to 0.5
- coarse_edge_in: bfloat16 [2, 384, 128], replicated, may hold values from -0.3125 to 0.3125
- coarse_edge_out: bfloat16 [2, 128, 128], replicated, may hold values from -0.5 to 0.5
- coarse_node_in: bfloat16 [2, 256, 128], replicated, may hold values from -0.375 to 0.375
- coarse_node_out: bfloat16 [2, 128, 128], replicated, may hold values from -0.5 to 0.5
Outputs:
- new_state: bfloat16 [131072, 128], P(('fine', 'coarse'))
- state_grad: bfloat16 [131072, 128], P(('fine', 'coarse'))
- grad_fine_edge_in: float32 [2, 384, 128], replicated
- grad_fine_edge_out: float32 [2, 128, 128], replicated
- grad_fine_node_in: float32 [2, 256, 128], replicated
- grad_fine_node_out: float32 [2, 128, 128], replicated
- grad_coarse_edge_in: float32 [2, 384, 128], replicated
- grad_coarse_edge_out: float32 [2, 128, 128], replicated
- grad_coarse_node_in: float32 [2, 256, 128], replicated
- grad_coarse_node_out: float32 [2, 128, 128], replicated
Inputs may be any that keep to these rules, and one draw needn't show every extreme that they name: `block_owner`: among the 64 blocks of one partition, at most 5 name the same owner, and in every draw some owner is named exactly 5 times.
All inputs are finite; a program needn't handle non-finite values.
Results may differ from a plain program's by a relative error of at most 0.039.
Values may be sent and summed in bfloat16 or wider, within the bound.
A program may use at most 128 MiB of HBM per device.

v0:
```python
import jax
import jax.numpy as jnp
from jax import lax
from jax.sharding import PartitionSpec as P

POOL = 16


norm_eps = 1e-05


def padded_2(x, sides, width):
    for axis, dim in sides:
        count, length = (lax.axis_size(axis), x.shape[dim])
        up = [(i, (i + 1) % count) for i in range(count)]
        down = [(j, i) for i, j in up]
        last = lax.slice_in_dim(x, length - width, length, axis=dim)
        first = lax.slice_in_dim(x, 0, width, axis=dim)
        before = lax.ppermute(last, axis, up)
        after = lax.ppermute(first, axis, down)
        x = jnp.concatenate([before, x, after], axis=dim)
    return x


def normalize(values):
    center = values - jnp.mean(values, axis=-1, keepdims=True)
    spread = jnp.mean(center * center, axis=-1, keepdims=True)
    return center * lax.rsqrt(spread + norm_eps)


def perceptron(inputs, w_first, w_second):
    hidden = jax.nn.silu(jnp.dot(inputs, w_first, preferred_element_type=jnp.float32)).astype(
        jnp.bfloat16
    )
    return normalize(jnp.dot(hidden, w_second, preferred_element_type=jnp.float32))


def graph_layer(
    state, extra, edges, senders, receivers, live, w_edge_in, w_edge_out, w_node_in, w_node_out
):
    table = jnp.concatenate([state, extra], axis=0)
    joined = jnp.concatenate([edges, table[senders], state[receivers]], axis=1)
    new_edges = (edges.astype(jnp.float32) + perceptron(joined, w_edge_in, w_edge_out)).astype(
        jnp.bfloat16
    )
    incoming = jax.ops.segment_sum(
        new_edges.astype(jnp.float32), receivers, num_segments=state.shape[0]
    ).astype(jnp.bfloat16)
    node_input = jnp.concatenate([state, incoming], axis=1)
    updated = state.astype(jnp.float32) + perceptron(node_input, w_node_in, w_node_out)
    if live is not None:
        updated = updated * live
    return (updated.astype(jnp.bfloat16), new_edges)


def slot_table(owners, groups, capacity):
    choose = (owners[:, None] == jnp.arange(groups, dtype=jnp.int32)[None, :]).astype(jnp.int32)
    ranks = jnp.sum((jnp.cumsum(choose, axis=0) - 1) * choose, axis=1)
    places = owners * capacity + ranks
    return (places[:, None] == jnp.arange(groups * capacity, dtype=jnp.int32)[None, :]).astype(
        jnp.bfloat16
    )


def pool_rows(state, select, pool_size):
    width = state.shape[1]
    pooled = jnp.mean(state.astype(jnp.float32).reshape(-1, pool_size, width), axis=1).astype(
        jnp.bfloat16
    )
    placed = lax.dot_general(
        select, pooled, (((0,), (0,)), ((), ())), preferred_element_type=jnp.float32
    )
    return placed.astype(jnp.bfloat16)


def prolong(state, back, select, pool_size):
    width = state.shape[1]
    picked = jnp.dot(select, back, preferred_element_type=jnp.float32)
    grown = state.astype(jnp.float32).reshape(-1, pool_size, width) + picked[:, None, :]
    return grown.reshape(state.shape).astype(jnp.bfloat16)


def add_three(first, second, third):
    return (
        first.astype(jnp.float32) + second.astype(jnp.float32) + third.astype(jnp.float32)
    ).astype(jnp.bfloat16)


def add_two(first, second):
    return (first.astype(jnp.float32) + second.astype(jnp.float32)).astype(jnp.bfloat16)


def fine_rows(values):
    return lax.all_to_all(values, "fine", split_axis=0, concat_axis=0, tiled=True)


def coarse_rows(values):
    return lax.all_to_all(values, "coarse", split_axis=0, concat_axis=0, tiled=True)


def cycle(values):
    return padded_2(values, (("coarse", 0),), 1)


def body(
    node_state,
    fine_edge_state,
    coarse_edge_state,
    fine_src,
    fine_dst,
    halo_rows,
    block_owner,
    coarse_src,
    coarse_dst,
    cotangent,
    fine_edge_in,
    fine_edge_out,
    fine_node_in,
    fine_node_out,
    coarse_edge_in,
    coarse_edge_out,
    coarse_node_in,
    coarse_node_out,
):
    width = node_state.shape[1]
    groups = lax.axis_size("coarse")
    blocks = node_state.shape[0] // POOL
    capacity = max(2, 5 * blocks // (2 * groups))
    slots = groups * capacity
    select = slot_table(block_owner[:, 0], groups, capacity)
    flags = jnp.sum(select, axis=0).astype(jnp.int32).reshape(groups, capacity)

    def pick(state):
        return state[halo_rows.reshape(-1)].reshape(halo_rows.shape[0], halo_rows.shape[1], width)

    def pick_back(state, grad):
        return jax.vjp(pick, state)[1](grad)[0]

    def fine_step(state, received, edges, w_a, w_b, w_c, w_d):
        return graph_layer(
            state, received.reshape(-1, width), edges, fine_src, fine_dst, None, w_a, w_b, w_c, w_d
        )

    def neighbours(states):
        padded = cycle(states[None])
        return jnp.concatenate([padded[0], padded[2]], axis=0)

    def neighbours_back(grad_extra, grad_state):
        padded = cycle(jnp.stack([grad_extra[:slots], grad_extra[slots:]]))
        return add_three(grad_state, padded[0], padded[3])

    recv_one = fine_rows(pick(node_state))
    (state_one, edges_one), fine_pull_a = jax.vjp(
        fine_step,
        node_state,
        recv_one,
        fine_edge_state,
        fine_edge_in[0],
        fine_edge_out[0],
        fine_node_in[0],
        fine_node_out[0],
    )

    def pool_step(state):
        return pool_rows(state, select, POOL)

    placed, pool_pull = jax.vjp(pool_step, state_one)
    arrived, arrived_flags = (
        lax.all_to_all(
            placed.reshape(groups, capacity, width),
            "coarse",
            split_axis=0,
            concat_axis=0,
            tiled=True,
        ),
        lax.all_to_all(flags, "coarse", split_axis=0, concat_axis=0, tiled=True),
    )
    coarse_zero = arrived.reshape(slots, width)
    live = arrived_flags.reshape(slots, 1).astype(jnp.float32)

    def coarse_step(state, extra, edges, w_a, w_b, w_c, w_d):
        return graph_layer(state, extra, edges, coarse_src, coarse_dst, live, w_a, w_b, w_c, w_d)

    extra_zero = neighbours(coarse_zero)
    (coarse_one, cedges_one), coarse_pull_a = jax.vjp(
        coarse_step,
        coarse_zero,
        extra_zero,
        coarse_edge_state,
        coarse_edge_in[0],
        coarse_edge_out[0],
        coarse_node_in[0],
        coarse_node_out[0],
    )
    extra_one = neighbours(coarse_one)
    (coarse_two, cedges_two), coarse_pull_b = jax.vjp(
        coarse_step,
        coarse_one,
        extra_one,
        cedges_one,
        coarse_edge_in[1],
        coarse_edge_out[1],
        coarse_node_in[1],
        coarse_node_out[1],
    )
    back = coarse_rows(coarse_two.reshape(groups, capacity, width)).reshape(slots, width)

    def prolong_step(state, value):
        return prolong(state, value, select, POOL)

    state_two, prolong_pull = jax.vjp(prolong_step, state_one, back)
    recv_two = fine_rows(pick(state_two))
    (new_state, edges_two), fine_pull_b = jax.vjp(
        fine_step,
        state_two,
        recv_two,
        edges_one,
        fine_edge_in[1],
        fine_edge_out[1],
        fine_node_in[1],
        fine_node_out[1],
    )
    grads_late = fine_pull_b((cotangent, jnp.zeros_like(edges_two)))
    grad_two = add_two(grads_late[0], pick_back(state_two, fine_rows(grads_late[1])))
    grad_one_local, grad_back = prolong_pull(grad_two)
    grad_ctwo = coarse_rows(grad_back.reshape(groups, capacity, width)).reshape(slots, width)
    grads_cb = coarse_pull_b((grad_ctwo, jnp.zeros_like(cedges_two)))
    grad_cone = neighbours_back(grads_cb[1], grads_cb[0])
    grads_ca = coarse_pull_a((grad_cone, grads_cb[2]))
    grad_czero = neighbours_back(grads_ca[1], grads_ca[0])
    grad_placed = coarse_rows(grad_czero.reshape(groups, capacity, width)).reshape(slots, width)
    grad_one = add_two(grad_one_local, pool_pull(grad_placed)[0])
    grads_early = fine_pull_a((grad_one, grads_late[2]))
    state_grad = add_two(grads_early[0], pick_back(node_state, fine_rows(grads_early[1])))

    def paired(first, second):
        return jnp.stack([first, second]).astype(jnp.float32)

    g_fei = paired(grads_early[3], grads_late[3])
    g_feo = paired(grads_early[4], grads_late[4])
    g_fni = paired(grads_early[5], grads_late[5])
    g_fno = paired(grads_early[6], grads_late[6])
    g_cei = paired(grads_ca[3], grads_cb[3])
    g_ceo = paired(grads_ca[4], grads_cb[4])
    g_cni = paired(grads_ca[5], grads_cb[5])
    g_cno = paired(grads_ca[6], grads_cb[6])
    summed = lax.psum((g_fei, g_feo, g_fni, g_fno, g_cei, g_ceo, g_cni, g_cno), ("fine", "coarse"))
    return (
        new_state,
        state_grad,
        summed[0],
        summed[1],
        summed[2],
        summed[3],
        summed[4],
        summed[5],
        summed[6],
        summed[7],
    )


def solution(mesh):
    placed = (
        P(("fine", "coarse"), None),
        P(("fine", "coarse"), None),
        P(("fine", "coarse"), None),
        P(("fine", "coarse")),
        P(("fine", "coarse")),
        P(("fine", "coarse"), None),
        P(("fine", "coarse"), None),
        P(("fine", "coarse")),
        P(("fine", "coarse")),
        P(("fine", "coarse"), None),
        P(),
        P(),
        P(),
        P(),
        P(),
        P(),
        P(),
        P(),
    )
    return jax.shard_map(
        body,
        mesh=mesh,
        in_specs=placed,
        out_specs=(
            P(("fine", "coarse"), None),
            P(("fine", "coarse"), None),
            P(),
            P(),
            P(),
            P(),
            P(),
            P(),
            P(),
            P(),
        ),
        check_vma=False,
    )
```

profile of v0, /device:TPU:1, one launch (start us, length us, event | category | flops | bytes accessed | tf_op | source)
XLA Modules:
  0.0 652.2 jit_solution(11507429608732240036)
XLA Ops:
  23.3 12.1 %gather_fusion.2 = bf16[4096,128]{1,0:T(8,128)(2,1)S(1)} fusion(bf16[1024,128]{1,0:T(8,128)(2,1)S(1)} %copy-done, s32[4096]{0:T(1024)S(1)} %get-tuple-element.52), kind=kCustom, calls=%fused_computation.2 | custom fusion | bytes 2113536 | tf_op jit(solution)/shard_map/jvp()/gather | solution.py:42
  36.1 12.1 %gather_fusion.1 = bf16[4096,128]{1,0:T(8,128)(2,1)S(1)} fusion(bf16[1536,128]{1,0:T(8,128)(2,1)S(1)} %pad_maximum_fusion.10, s32[4096]{0:T(1024)S(1)} %get-tuple-element.55), kind=kCustom, calls=%fused_computation.1 | custom fusion | bytes 2113536 | tf_op jit(solution)/shard_map/jvp()/gather | solution.py:42
  58.8 22.8 %scatter_custom_fusion = f32[1024,128]{1,0:T(8,128)S(1)} fusion(s32[4096]{0:T(1024)S(1)} %copy-done.91, f32[4096,128]{1,0:T(8,128)} %copy.79, f32[]{:T(128)} %constant.90.clone.1), kind=kCustom, calls=%fused_computation.218 | custom fusion | flops 524288 | bytes 524800 | tf_op jit(solution)/shard_map/jvp()/scatter-add | solution.py:46
  85.5 10.6 %all-to-all-start.1 = ((bf16[32,5,128]{2,1,0:T(8,128)(2,1)}), bf16[32,5,128]{2,1,0:T(8,128)(2,1)S(1)}, u32[]{:S(2)}, u32[]{:S(2)}) async-start(bf16[32,5,128]{2,1,0:T(8,128)(2,1)} %reshape.359), calls=%async_computation.1 | async-start | bytes 131072 | tf_op jit(solution)/shard_map/all_to_all | solution.py:169
  96.8 8.1 %all-to-all-done.1 = bf16[32,5,128]{2,1,0:T(8,128)(2,1)S(1)} async-done(((bf16[32,5,128]{2,1,0:T(8,128)(2,1)}), bf16[32,5,128]{2,1,0:T(8,128)(2,1)S(1)}, u32[]{:S(2)}, u32[]{:S(2)}) %all-to-all-start.1) | async-done | bytes 40992 | tf_op jit(solution)/shard_map/all_to_all | solution.py:169
  109.0 7.1 %collective-permute-start.1 = (bf16[1,160,128]{2,1,0:T(8,128)(2,1)S(1)}, bf16[1,160,128]{2,1,0:T(8,128)(2,1)S(1)}, u32[]{:S(2)}, u32[]{:S(2)}) collective-permute-start(bf16[1,160,128]{2,1,0:T(8,128)(2,1)S(1)} %broadcast_in_dim_reshape.3), channel_id=1, source_target_pairs={{1,0},{2,1},{3,2},{4,3},{5,4},{6,5},{7,6},{8,7},{9,8},{10,9},{11,1... | collective-permute-start | bytes 122888 | tf_op jit(solution)/shard_map/ppermute | solution.py:20
  163.7 8.3 %all-to-all-done.3 = bf16[32,5,128]{2,1,0:T(8,128)(2,1)S(1)} async-done(((bf16[32,5,128]{2,1,0:T(8,128)(2,1)}), bf16[32,5,128]{2,1,0:T(8,128)(2,1)S(1)}, u32[]{:S(2)}, u32[]{:S(2)}) %all-to-all-start.3) | async-done | bytes 40992 | tf_op jit(solution)/shard_map/all_to_all | solution.py:98
  174.5 19.6 %all-to-all-start.4 = ((bf16[4,128,128]{2,1,0:T(8,128)(2,1)}), bf16[4,128,128]{2,1,0:T(8,128)(2,1)S(1)}, u32[]{:S(2)}, u32[]{:S(2)}) async-start(bf16[4,128,128]{2,1,0:T(8,128)(2,1)} %bitcast.27), calls=%async_computation.4 | async-start | bytes 262144 | tf_op jit(solution)/shard_map/all_to_all | solution.py:94
  194.7 14.9 %gather_fusion.9 = bf16[4096,128]{1,0:T(8,128)(2,1)} fusion(bf16[1024,128]{1,0:T(8,128)(2,1)S(1)} %fusion.70, s32[4096]{0:T(1024)S(1)} %get-tuple-element.52), kind=kCustom, calls=%fused_computation.9 | custom fusion | bytes 2113536 | tf_op jit(solution)/shard_map/jvp()/gather | solution.py:42
  211.9 14.9 %gather_fusion.8 = bf16[4096,128]{1,0:T(8,128)(2,1)} fusion(bf16[1536,128]{1,0:T(8,128)(2,1)S(1)} %pad_maximum_fusion.11, s32[4096]{0:T(1024)S(1)} %get-tuple-element.55), kind=kCustom, calls=%fused_computation.8 | custom fusion | bytes 2113536 | tf_op jit(solution)/shard_map/jvp()/gather | solution.py:42
  239.0 23.4 %scatter_custom_fusion.3 = f32[1024,128]{1,0:T(8,128)} fusion(s32[4096]{0:T(1024)} %param.22, f32[4096,128]{1,0:T(8,128)} %copy.88, f32[]{:T(128)} %constant.90.clone.1), kind=kCustom, calls=%fused_computation.216 | custom fusion | flops 524288 | bytes 524800 | tf_op jit(solution)/shard_map/jvp()/scatter-add | solution.py:46
  277.4 16.2 %gather_fusion.10 = bf16[4096,128]{1,0:T(8,128)(2,1)} fusion(bf16[1024,128]{1,0:T(8,128)(2,1)S(1)} %split.153, s32[4096]{0:T(1024)} %get-tuple-element.53), kind=kCustom, calls=%fused_computation.10 | custom fusion | bytes 2113536 | tf_op jit(solution)/shard_map/transpose(jvp())/gather | solution.py:46
  308.9 22.9 %scatter_custom_fusion.4 = bf16[1536,128]{1,0:T(8,128)(2,1)S(1)} fusion(s32[4096]{0:T(1024)} %get-tuple-element.54, bf16[4096,128]{1,0:T(8,128)(2,1)} %copy.91, bf16[]{:T(256)} %constant.102.clone.1), kind=kCustom, calls=%fused_computation.224 | custom fusion | flops 524288 | bytes 393728 | tf_op jit(solution)/shard_map/transpose(jvp())/scatter-add | solution.py:42
  340.7 23.0 %scatter_fusion = bf16[1024,128]{1,0:T(8,128)(2,1)S(1)} fusion(bf16[1024,128]{1,0:T(8,128)(2,1)S(1)} %slice_add_fusion.3, s32[4096]{0:T(1024)S(1)} %copy-done.90, bf16[4096,128]{1,0:T(8,128)(2,1)S(1)} %copy.92), kind=kCustom, calls=%fused_computation.19 | custom fusion | flops 524288 | bytes 3162112 | tf_op jit(solution)/shard_map/transpose(jvp())/scatter-add | solution.py:42
  373.6 7.9 %all-to-all-done.6 = bf16[32,5,128]{2,1,0:T(8,128)(2,1)S(1)} async-done(((bf16[32,5,128]{2,1,0:T(8,128)(2,1)}), bf16[32,5,128]{2,1,0:T(8,128)(2,1)S(1)}, u32[]{:S(2)}, u32[]{:S(2)}) %all-to-all-start.6) | async-done | bytes 40992 | tf_op jit(solution)/shard_map/all_to_all | solution.py:98
  414.2 6.6 %scatter_custom_fusion.9 = bf16[480,128]{1,0:T(8,128)(2,1)S(1)} fusion(s32[640]{0:T(1024)} %compare_select_fusion.4, bf16[640,384]{1,0:T(8,128)(2,1)S(1)} %convolution_convert_fusion.6, bf16[]{:T(256)} %constant.102.clone.1), kind=kCustom, calls=%fused_computation.230 | custom fusion | flops 81920 | bytes 287232 | tf_op jit(solution)/shard_map/transpose(jvp())/scatter-add | solution.py:42
  420.9 7.2 %collective-permute-start.7 = (bf16[1,160,128]{2,1,0:T(8,128)(2,1)S(1)}, bf16[1,160,128]{2,1,0:T(8,128)(2,1)S(1)}, u32[]{:S(2)}, u32[]{:S(2)}) collective-permute-start(bf16[1,160,128]{2,1,0:T(8,128)(2,1)S(1)} %get-tuple-element.46), channel_id=1, source_target_pairs={{1,0},{2,1},{3,2},{4,3},{5,4},{6,5},{7,6},{8,7},{9,8},{10,9},{11,1... | collective-permute-start | bytes 122888 | tf_op jit(solution)/shard_map/ppermute | solution.py:20
  430.3 6.4 scatter_custom_fusion.10
  442.2 7.9 %all-to-all-done.7 = bf16[32,5,128]{2,1,0:T(8,128)(2,1)S(1)} async-done(((bf16[32,5,128]{2,1,0:T(8,128)(2,1)}), bf16[32,5,128]{2,1,0:T(8,128)(2,1)S(1)}, u32[]{:S(2)}, u32[]{:S(2)}) %all-to-all-start.7) | async-done | bytes 40992 | tf_op jit(solution)/shard_map/all_to_all | solution.py:98
  455.0 14.9 %gather_fusion.13 = bf16[4096,128]{1,0:T(8,128)(2,1)} fusion(bf16[1024,128]{1,0:T(8,128)(2,1)S(1)} %split.152, s32[4096]{0:T(1024)S(1)} %copy-done.70), kind=kCustom, calls=%fused_computation.13 | custom fusion | bytes 2113536 | tf_op jit(solution)/shard_map/transpose(jvp())/gather | solution.py:46
  485.5 23.4 %scatter_custom_fusion.11 = bf16[1536,128]{1,0:T(8,128)(2,1)} fusion(s32[4096]{0:T(1024)} %get-tuple-element.54, bf16[4096,384]{1,0:T(8,128)(2,1)S(1)} %convolution_convert_fusion, bf16[]{:T(256)} %constant.102.clone.1), kind=kCustom, calls=%fused_computation.128 | custom fusion | flops 524288 | bytes 1442304 | tf_op jit(solution)/shard_map/transpose(jvp())/scatter-add | solution.py:42
  510.5 7.6 %all-to-all-start.8 = ((bf16[4,128,128]{2,1,0:T(8,128)(2,1)}), bf16[4,128,128]{2,1,0:T(8,128)(2,1)S(1)}, u32[]{:S(2)}, u32[]{:S(2)}) async-start(bf16[4,128,128]{2,1,0:T(8,128)(2,1)} %bitcast.45), calls=%async_computation.8 | async-start | bytes 262144 | tf_op jit(solution)/shard_map/all_to_all | solution.py:94
  519.9 21.8 %scatter_custom_fusion.12 = bf16[1024,128]{1,0:T(8,128)(2,1)} fusion(bf16[1024,128]{1,0:T(8,128)(2,1)} %slice_add_fusion.1, s32[4096]{0:T(1024)S(1)} %copy-done.90, bf16[4096,384]{1,0:T(8,128)(2,1)S(1)} %convolution_convert_fusion), kind=kCustom, calls=%fused_computation.126 | custom fusion | flops 524288 | bytes 1310720 | tf_op jit(solution)/shard_map/transpose(jvp())/scatter-add | solution.py:42
  547.1 88.4 %all-reduce.3.cloned.1.call-done = (f32[2,384,128]{2,1,0:T(8,128)}, f32[2,128,128]{2,1,0:T(8,128)}, f32[2,256,128]{2,1,0:T(8,128)}, f32[2,128,128]{2,1,0:T(8,128...) async-done(((f32[2,384,128]{2,1,0:T(8,128)}, f32[2,128,128]{2,1,0:T(8,128)}, f32[2,256,128]{2,1,0:T(8,128)}, ...) | async-done | bytes 1835024 | tf_op jit(solution)/shard_map/psum | solution.py:247
  (571 shorter events, 226.9 us)
Async XLA Ops:
  11.9 24.2 %all-to-all-start = ((bf16[4,128,128]{2,1,0:T(8,128)(2,1)}), bf16[4,128,128]{2,1,0:T(8,128)(2,1)S(1)}, u32[]{:S(2)}, u32[]{:S(2)}) async-start(bf16[4,128,128]{2,1,0:T(8,128)(2,1)} %bitcast.2), calls=%async_computation | async-start | bytes 262144 | tf_op jit(solution)/shard_map/all_to_all | solution.py:94
  57.1 172.0 %copy-start.7 = (bf16[4096,128]{0,1:T(8,128)(2,1)}, bf16[4096,128]{0,1:T(8,128)(2,1)S(1)}, u32[]{:S(2)}) copy-start(bf16[4096,128]{0,1:T(8,128)(2,1)S(1)} %add_convert_fusion.1) | copy-start | bytes 3145732
  83.2 89.0 %copy-start.75 = (f32[1024]{0:T(1024)}, f32[1024]{0:T(1024)S(1)}, u32[]{:S(2)}) copy-start(f32[1024]{0:T(1024)S(1)} %broadcast_multiply_fusion.5) | copy-start | bytes 12292
  84.1 88.0 %copy-start.94 = (f32[1024]{0:T(1024)}, f32[1024]{0:T(1024)S(1)}, u32[]{:S(2)}) copy-start(f32[1024]{0:T(1024)S(1)} %fusion.228) | copy-start | bytes 12292
  85.5 19.5 %all-to-all-start.1 = ((bf16[32,5,128]{2,1,0:T(8,128)(2,1)}), bf16[32,5,128]{2,1,0:T(8,128)(2,1)S(1)}, u32[]{:S(2)}, u32[]{:S(2)}) async-start(bf16[32,5,128]{2,1,0:T(8,128)(2,1)} %reshape.359), calls=%async_computation.1 | async-start | bytes 131072 | tf_op jit(solution)/shard_map/all_to_all | solution.py:169
  104.9 12.4 %all-to-all-start.2 = ((s32[32,1,5]{2,1,0:T(1,128)}), s32[32,1,5]{2,1,0:T(1,128)S(1)}, u32[]{:S(2)}, u32[]{:S(2)}) async-start(s32[32,1,5]{2,1,0:T(1,128)} %bitcast.18), calls=%async_computation.2 | async-start | bytes 32768 | tf_op jit(solution)/shard_map/all_to_all | solution.py:176
  109.0 10.5 %collective-permute-start.1 = (bf16[1,160,128]{2,1,0:T(8,128)(2,1)S(1)}, bf16[1,160,128]{2,1,0:T(8,128)(2,1)S(1)}, u32[]{:S(2)}, u32[]{:S(2)}) collective-permute-start(bf16[1,160,128]{2,1,0:T(8,128)(2,1)S(1)} %broadcast_in_dim_reshape.3), channel_id=1, source_target_pairs={{1,0},{2,1},{3,2},{4,3},{5,4},{6,5},{7,6},{8,7},{9,8},{10,9},{11,1... | collective-permute-start | bytes 122888 | tf_op jit(solution)/shard_map/ppermute | solution.py:20
  116.1 8.8 %collective-permute-start = (bf16[1,160,128]{2,1,0:T(8,128)(2,1)S(1)}, bf16[1,160,128]{2,1,0:T(8,128)(2,1)S(1)}, u32[]{:S(2)}, u32[]{:S(2)}) collective-permute-start(bf16[1,160,128]{2,1,0:T(8,128)(2,1)S(1)} %broadcast_in_dim_reshape.3), channel_id=1, source_target_pairs={{0,1},{1,2},{2,3},{3,4},{4,5},{5,6},{6,7},{7,8},{8,9},{9,10},{10,1... | collective-permute-start | bytes 122888 | tf_op jit(solution)/shard_map/ppermute | solution.py:19
  137.6 3.7 collective-permute-start.3
  138.5 8.6 %collective-permute-start.2 = (bf16[1,160,128]{2,1,0:T(8,128)(2,1)S(1)}, bf16[1,160,128]{2,1,0:T(8,128)(2,1)S(1)}, u32[]{:S(2)}, u32[]{:S(2)}) collective-permute-start(bf16[1,160,128]{2,1,0:T(8,128)(2,1)S(1)} %bitcast.210), channel_id=1, source_target_pairs={{0,1},{1,2},{2,3},{3,4},{4,5},{5,6},{6,7},{7,8},{8,9},{9,10},{10,1... | collective-permute-start | bytes 122888 | tf_op jit(solution)/shard_map/ppermute | solution.py:19
  157.8 51.8 %copy-start.59 = (bf16[160,128]{1,0:T(8,128)(2,1)}, bf16[160,128]{1,0:T(8,128)(2,1)S(1)}, u32[]{:S(2)}) copy-start(bf16[160,128]{1,0:T(8,128)(2,1)S(1)} %convert_element_type.456) | copy-start | bytes 122884
  157.9 51.6 %copy-start.88 = (f32[160,128]{1,0:T(8,128)}, f32[160,128]{1,0:T(8,128)S(1)}, u32[]{:S(2)}) copy-start(f32[160,128]{1,0:T(8,128)S(1)} %fusion.147) | copy-start | bytes 245764
  158.2 51.4 %copy-start.31 = (f32[160,128]{1,0:T(8,128)}, f32[160,128]{1,0:T(8,128)S(1)}, u32[]{:S(2)}) copy-start(f32[160,128]{1,0:T(8,128)S(1)} %get-tuple-element.69) | copy-start | bytes 245764
  159.2 12.7 %all-to-all-start.3 = ((bf16[32,5,128]{2,1,0:T(8,128)(2,1)}), bf16[32,5,128]{2,1,0:T(8,128)(2,1)S(1)}, u32[]{:S(2)}, u32[]{:S(2)}) async-start(bf16[32,5,128]{2,1,0:T(8,128)(2,1)} %reshape.361), calls=%async_computation.3 | async-start | bytes 131072 | tf_op jit(solution)/shard_map/all_to_all | solution.py:98
  174.5 37.4 %all-to-all-start.4 = ((bf16[4,128,128]{2,1,0:T(8,128)(2,1)}), bf16[4,128,128]{2,1,0:T(8,128)(2,1)S(1)}, u32[]{:S(2)}, u32[]{:S(2)}) async-start(bf16[4,128,128]{2,1,0:T(8,128)(2,1)} %bitcast.27), calls=%async_computation.4 | async-start | bytes 262144 | tf_op jit(solution)/shard_map/all_to_all | solution.py:94
  333.5 30.3 %all-to-all-start.5 = ((bf16[4,128,128]{2,1,0:T(8,128)(2,1)}), bf16[4,128,128]{2,1,0:T(8,128)(2,1)}, u32[]{:S(2)}, u32[]{:S(2)}) async-start(bf16[4,128,128]{2,1,0:T(8,128)(2,1)} %bitcast.33), calls=%async_computation.5 | async-start | bytes 262144 | tf_op jit(solution)/shard_map/all_to_all | solution.py:94
  368.7 12.7 %all-to-all-start.6 = ((bf16[32,5,128]{2,1,0:T(8,128)(2,1)}), bf16[32,5,128]{2,1,0:T(8,128)(2,1)S(1)}, u32[]{:S(2)}, u32[]{:S(2)}) async-start(bf16[32,5,128]{2,1,0:T(8,128)(2,1)} %reshape.368), calls=%async_computation.6 | async-start | bytes 131072 | tf_op jit(solution)/shard_map/all_to_all | solution.py:98
  396.1 8.5 %collective-permute-start.5 = (bf16[1,160,128]{2,1,0:T(8,128)(2,1)}, bf16[1,160,128]{2,1,0:T(8,128)(2,1)S(1)}, u32[]{:S(2)}, u32[]{:S(2)}) collective-permute-start(bf16[1,160,128]{2,1,0:T(8,128)(2,1)} %get-tuple-element.49), channel_id=1, source_target_pairs={{1,0},{2,1},{3,2},{4,3},{5,4},{6,5},{7,6},{8,7},{9,8},{10,9},{11,1... | collective-permute-start | bytes 122888 | tf_op jit(solution)/shard_map/ppermute | solution.py:20
  397.9 8.8 %collective-permute-start.4 = (bf16[1,160,128]{2,1,0:T(8,128)(2,1)}, bf16[1,160,128]{2,1,0:T(8,128)(2,1)S(1)}, u32[]{:S(2)}, u32[]{:S(2)}) collective-permute-start(bf16[1,160,128]{2,1,0:T(8,128)(2,1)} %get-tuple-element.50), channel_id=1, source_target_pairs={{0,1},{1,2},{2,3},{3,4},{4,5},{5,6},{6,7},{7,8},{8,9},{9,10},{10,1... | collective-permute-start | bytes 122888 | tf_op jit(solution)/shard_map/ppermute | solution.py:19
  420.9 15.9 %collective-permute-start.6 = (bf16[1,160,128]{2,1,0:T(8,128)(2,1)S(1)}, bf16[1,160,128]{2,1,0:T(8,128)(2,1)S(1)}, u32[]{:S(2)}, u32[]{:S(2)}) collective-permute-start(bf16[1,160,128]{2,1,0:T(8,128)(2,1)S(1)} %get-tuple-element.45), channel_id=1, source_target_pairs={{0,1},{1,2},{2,3},{3,4},{4,5},{5,6},{6,7},{7,8},{8,9},{9,10},{10,1... | collective-permute-start | bytes 122888 | tf_op jit(solution)/shard_map/ppermute | solution.py:19
  420.9 15.8 %collective-permute-start.7 = (bf16[1,160,128]{2,1,0:T(8,128)(2,1)S(1)}, bf16[1,160,128]{2,1,0:T(8,128)(2,1)S(1)}, u32[]{:S(2)}, u32[]{:S(2)}) collective-permute-start(bf16[1,160,128]{2,1,0:T(8,128)(2,1)S(1)} %get-tuple-element.46), channel_id=1, source_target_pairs={{1,0},{2,1},{3,2},{4,3},{5,4},{6,5},{7,6},{8,7},{9,8},{10,9},{11,1... | collective-permute-start | bytes 122888 | tf_op jit(solution)/shard_map/ppermute | solution.py:20
  437.4 12.7 %all-to-all-start.7 = ((bf16[32,5,128]{2,1,0:T(8,128)(2,1)}), bf16[32,5,128]{2,1,0:T(8,128)(2,1)S(1)}, u32[]{:S(2)}, u32[]{:S(2)}) async-start(bf16[32,5,128]{2,1,0:T(8,128)(2,1)} %reshape.369), calls=%async_computation.7 | async-start | bytes 131072 | tf_op jit(solution)/shard_map/all_to_all | solution.py:98
  441.3 194.2 %all-reduce.3.cloned.1.call-start = ((), (), s32[]{:S(2)}) async-start(), calls=%async_computation.9 | async-start | bytes 3670016 | tf_op jit(solution)/shard_map/psum | solution.py:247
  510.5 31.2 %all-to-all-start.8 = ((bf16[4,128,128]{2,1,0:T(8,128)(2,1)}), bf16[4,128,128]{2,1,0:T(8,128)(2,1)S(1)}, u32[]{:S(2)}, u32[]{:S(2)}) async-start(bf16[4,128,128]{2,1,0:T(8,128)(2,1)} %bitcast.45), calls=%async_computation.8 | async-start | bytes 262144 | tf_op jit(solution)/shard_map/all_to_all | solution.py:94
  (156 other events, 1648.1 us)
Sparse Core Ops, SparseCore 0:
  483.4 152.0 all-reduce.2
where the time goes:
time: 662 us; the launch traced here: 652 us
  other arithmetic  218 us (33%)
  local copies, waits for them, and re-layouts  160 us (24%)
  waiting for transfers between devices  135 us (20%)
  starting transfers between devices  80.2 us (12%)
  matrix products  41.8 us (6%)
  between operations  17.1 us (3%)
    scatter-add x8, other arithmetic, graph_layer(): joined = jnp.concatenate([edges, table[senders], state[receivers]], axis=1)  117 us
    psum x1, waiting for transfers between devices, body(): lax.psum((g_fei, g_feo, g_fni, g_fno, g_cei, g_ceo, g_cni, g_cno), ('fine...  88.4 us
    gather x12, local copies, waits for them, and re-layouts, graph_layer(): joined = jnp.concatenate([edges, table[senders], state[receivers]], axis=1)  66.9 us
    scatter-add x4, other arithmetic, graph_layer(): jax.ops.segment_sum(new_edges.astype(jnp.float32), receivers, num_segment...  58.3 us
    gather x8, local copies, waits for them, and re-layouts, graph_layer(): jax.ops.segment_sum(new_edges.astype(jnp.float32), receivers, num_segment...  40.2 us
    all_to_all x4, starting transfers between devices, fine_rows(): lax.all_to_all(values, 'fine', split_axis=0, concat_axis=0, tiled=True)  36 us
    unnamed x338, local copies, waits for them, and re-layouts  31.9 us
    all_to_all x3, waiting for transfers between devices, coarse_rows(): lax.all_to_all(values, 'coarse', split_axis=0, concat_axis=0, tiled=True)  24 us
  transfers between devices with their start and end apart: 18, of which 9 were waited for; matrix products, arithmetic and copies ran while one was open for 22% of the time, Pallas kernels for 0%

commit v1 on v0

v1 whole, which is shorter than its diff:
```python
from types import SimpleNamespace

import jax
import jax.numpy as jnp
from jax import lax
from jax.experimental import pallas as pl
from jax.experimental.pallas import tpu as pltpu
from jax.sharding import PartitionSpec as P

BF = jnp.bfloat16
F32 = jnp.float32
I16 = jnp.int16
I32 = jnp.int32
F8 = jnp.float8_e4m3fn
MESH = pl.DeviceIdType.MESH

L = 128
NF, EF, HALO = 1024, 4096, 512
NC, EC = 160, 640
BLOCKS, POOL, CAP = 64, 16, 5
PAD = 16
N_FINE, N_COARSE = 4, 32
WIDE = N_COARSE * PAD
SET = 896
PART = SET // N_FINE
OWNERS = PART // 8
EPS = 1e-05


def dot(a, b):
    return jnp.dot(a, b, preferred_element_type=F32)


def dot_nt(a, b):
    return lax.dot_general(a, b, (((1,), (1,)), ((), ())), preferred_element_type=F32)


def dot_tn(a, b):
    return lax.dot_general(a, b, (((0,), (0,)), ((), ())), preferred_element_type=F32)


def iota(shape, dim):
    return lax.broadcasted_iota(I32, shape, dim)


def ones_where(mask):
    return jnp.where(mask, jnp.asarray(1, BF), jnp.asarray(0, BF))


def lane_sum(x):
    return jnp.sum(x, axis=-1, keepdims=True)


def normed(y):
    center = y - lane_sum(y) * (1.0 / L)
    scale = lax.rsqrt(lane_sum(center * center) * (1.0 / L) + EPS)
    return center * scale, scale


def normed_back(dn, n, scale):
    return scale * (dn - lane_sum(dn) * (1.0 / L) - n * (lane_sum(dn * n) * (1.0 / L)))


def hot_columns(column, base, width, dtype):
    count = column.shape[0]
    lanes = iota((16, 128), 1).astype(I16)
    parts = []
    for start in range(0, width, 128):
        places = jnp.concatenate([lanes + jnp.asarray(base + start, I16)] * (count // 16), axis=0)
        parts.append(ones_where(column == places))
    hot = jnp.concatenate(parts, axis=1) if len(parts) > 1 else parts[0]
    return hot.astype(dtype)


def gather_rows(columns, table):
    total = None
    for column, base, width in columns:
        for k in range(0, width, 256):
            size = min(256, width - k)
            part = dot(hot_columns(column, k, size, table.dtype), table[base + k : base + k + size, :])
            total = part if total is None else total + part
    return total


def scatter_rows(rows_ref, data_ref, first, count, edges):
    down = iota((count, 128), 0).astype(I16)
    shift = jnp.asarray(first, I32).astype(I16)
    total = None
    for k in range(0, edges, 256):
        size = min(256, edges - k)
        parts = []
        for j in range(k // 128, (k + size) // 128):
            row = rows_ref[j] - shift
            parts.append(ones_where(down == jnp.concatenate([row] * (count // 16), axis=0)))
        hot = jnp.concatenate(parts, axis=1) if len(parts) > 1 else parts[0]
        part = dot(hot.astype(data_ref.dtype), data_ref[k : k + size, :])
        total = part if total is None else total + part
    return total


def column_peak(x):
    return jnp.max(jnp.abs(x), axis=0, keepdims=True)


def scale_for(peak):
    return jnp.exp2(7.0 - jnp.floor(jnp.log2(jnp.maximum(peak, 1e-30))))


def halves(x, scale):
    x = x * scale
    high = x.astype(F8)
    low = ((x - high.astype(F32)) * 16.0).astype(F8)
    return jnp.concatenate([high, low], axis=1)


def joined(pair, scale):
    return (pair[:, 0:L] + pair[:, L : 2 * L] * 0.0625) * (1.0 / scale)


def vm(*shape, dtype=F32):
    return pltpu.VMEM(shape, dtype)


def level_shapes(n, tab, own, e):
    def layer():
        return SimpleNamespace(
            tab=vm(tab, L, dtype=BF),
            slope=vm(e, L),
            hid=vm(e, L, dtype=BF),
            n=vm(e, L),
            scale=vm(e, L),
            e=vm(e, L, dtype=BF),
            g=vm(n, L, dtype=BF),
            slope2=vm(n, L),
            hid2=vm(n, L, dtype=BF),
            n2=vm(n, L),
            scale2=vm(n, L),
        )

    return SimpleNamespace(
        cs=vm(e, L, dtype=I16),
        cr=vm(e, L, dtype=I16),
        rs=vm(e // L, 16, L, dtype=I16),
        rr=vm(e // L, 16, L, dtype=I16),
        proj=vm(tab + own, L, dtype=BF),
        wide=vm(tab + own, L),
        proj8=vm(tab + own, 2 * L, dtype=F8),
        dz=vm(e, L, dtype=BF),
        e8=vm(e, 2 * L, dtype=F8),
        dg8=vm(own, 2 * L, dtype=F8),
        de=vm(e, L, dtype=BF),
        dg=vm(own, L, dtype=BF),
        acc=vm(n, L),
        layers=[layer(), layer()],
    )


def shapes():
    dma = pltpu.SemaphoreType.DMA
    return SimpleNamespace(
        f=level_shapes(NF, NF + HALO, NF, EF),
        c=level_shapes(NC, 512, 256, EC),
        state_one=vm(NF, L, dtype=BF),
        live=vm(NC, L),
        acc_b=vm(L, L),
        acc_e=vm(L, L),
        halo_col=vm(HALO, L, dtype=I16),
        halo_row=vm(HALO // L, 16, L, dtype=I16),
        grad_two=vm(NF, L, dtype=BF),
        grad_one=vm(NF, L, dtype=BF),
        grad_c=vm(NC, L, dtype=BF),
        place=[vm(BLOCKS, L, dtype=I32), vm(L, L, dtype=I32)],
        hs=[vm(HALO, L, dtype=BF) for _ in range(4)],
        hr=[vm(HALO, L, dtype=BF) for _ in range(2)],
        ws=[vm(WIDE, L, dtype=BF) for _ in range(4)],
        wr=[vm(WIDE, L, dtype=BF) for _ in range(4)],
        ns=[vm(2 * NC, L, dtype=BF) for _ in range(2)],
        nr=[vm(2 * NC, L, dtype=BF) for _ in range(2)],
        gw=vm(4, SET, L, dtype=BF),
        r1=vm(4, 3, PART, L, dtype=BF),
        p1=vm(4, PART, L),
        r2=vm(4, N_COARSE * 8, L),
        r3=vm(4, PART, L),
        r4=vm(4, SET, L),
        hs_sem=[dma((2, 3)) for _ in range(4)],
        ws_sem=[dma((2,)) for _ in range(4)],
        near_sem=[dma((2, 2)) for _ in range(4)],
        ar1_sem=dma((4, 2, 3)),
        ar2_sem=dma((4, 2)),
        ar3_sem=dma((4, 2)),
        ar4_sem=dma((4, 2, 3)),
    )


def flat(tree):
    if isinstance(tree, SimpleNamespace):
        return [leaf for part in vars(tree).values() for leaf in flat(part)]
    if isinstance(tree, list):
        return [leaf for part in tree for leaf in flat(part)]
    return [tree]


def rebuilt(tree, leaves):
    if isinstance(tree, SimpleNamespace):
        return SimpleNamespace(**{name: rebuilt(part, leaves) for name, part in vars(tree).items()})
    if isinstance(tree, list):
        return [rebuilt(part, leaves) for part in tree]
    return next(leaves)


def operands():
    def weights():
        return SimpleNamespace(ei=None, eo=None, ni=None, no=None)

    inputs = SimpleNamespace(
        node=None, edge=None, cedge=None, src=None, dst=None, halo=None, owner=None, csrc=None, cdst=None, cot=None,
        fw=weights(), cw=weights(),
    )
    outputs = SimpleNamespace(new_state=None, state_grad=None, fg=weights(), cg=weights())
    return inputs, outputs


STEPS = None


def kernel(*args):
    leaves = iter(args)
    I, O = (rebuilt(tree, leaves) for tree in operands())
    R = rebuilt(shapes(), leaves)
    f = lax.axis_index("fine")
    c = lax.axis_index("coarse")

    def fine_at(d):
        return lax.rem(f + d + N_FINE, N_FINE)

    def coarse_at(d):
        return lax.rem(c + d + N_COARSE, N_COARSE)

    def chunk(i, size, align=None):
        return pl.ds(pl.multiple_of(i * size, align or size), size)

    def remote(src, dst, send, recv, where):
        return pltpu.make_async_remote_copy(
            src_ref=src, dst_ref=dst, send_sem=send, recv_sem=recv, device_id=where, device_id_type=MESH
        )

    def wait_for(view, sem):
        pltpu.make_async_copy(view, view, sem).wait()

    barrier = pltpu.get_barrier_semaphore()

    def greet():
        for d in range(1, N_FINE):
            pl.semaphore_signal(barrier, inc=1, device_id=(fine_at(d), c), device_id_type=MESH)

        def one(d, carry):
            pl.semaphore_signal(barrier, inc=1, device_id=(f, coarse_at(d)), device_id_type=MESH)
            return carry

        lax.fori_loop(1, N_COARSE, one, 0)

    def spread(src, columns, rows, count):
        def one(j, carry):
            wide = jnp.broadcast_to(src[pl.ds(j, 1), :], (L, L))
            rows[j] = wide[:16, :].astype(I16)
            columns[chunk(j, L), :] = wide.T.astype(I16)
            return carry

        lax.fori_loop(0, count, one, 0)

    def halo_copies(src, dst, base, sem):
        out, back = [], []
        for d in range(1, N_FINE):
            q, at = fine_at(d), fine_at(-d)
            out.append(
                remote(
                    src.at[chunk(q, L), :],
                    dst.at[pl.ds(pl.multiple_of(base + f * L, L), L), :],
                    sem.at[0, d - 1],
                    sem.at[1, d - 1],
                    (q, c),
                )
            )
            back.append((dst.at[pl.ds(pl.multiple_of(base + at * L, L), L), :], sem.at[1, d - 1]))
        return out, back

    def halo_start(src, dst, base, sem):
        for copy in halo_copies(src, dst, base, sem)[0]:
            copy.start()
        dst[pl.ds(pl.multiple_of(base + f * L, L), L), :] = src[chunk(f, L), :]

    def halo_wait(src, dst, base, sem):
        out, back = halo_copies(src, dst, base, sem)
        for copy in out:
            copy.wait_send()
        for view, at in back:
            wait_for(view, at)

    def wide_start(k):
        src, dst, sem = R.ws[k], R.wr[k], R.ws_sem[k]

        def one(d, carry):
            o = coarse_at(d)
            remote(src.at[chunk(o, PAD), :], dst.at[chunk(c, PAD), :], sem.at[0], sem.at[1], (f, o)).start()
            return carry

        lax.fori_loop(1, N_COARSE, one, 0)
        dst[chunk(c, PAD), :] = src[chunk(c, PAD), :]

    def wide_wait(k):
        src, dst, sem = R.ws[k], R.wr[k], R.ws_sem[k]
        wait_for(src.at[pl.ds(0, WIDE - PAD), :], sem.at[0])
        wait_for(dst.at[pl.ds(0, WIDE - PAD), :], sem.at[1])

    def near_copies(up_src, up_dst, down_src, down_dst, sem):
        return (
            remote(up_src, up_dst, sem.at[0, 0], sem.at[1, 0], (f, coarse_at(1))),
            remote(down_src, down_dst, sem.at[0, 1], sem.at[1, 1], (f, coarse_at(-1))),
        )

    def sum_one_copies(s):
        out = []
        for d in range(1, N_FINE):
            q = fine_at(d)
            out.append(
                remote(
                    R.gw.at[s, chunk(q, PART, 32), :],
                    R.r1.at[s, d - 1],
                    R.ar1_sem.at[s, 0, d - 1],
                    R.ar1_sem.at[s, 1, d - 1],
                    (q, c),
                )
            )
        return out

    def sum_one(s):
        for copy in sum_one_copies(s):
            copy.start()

    def sum_two(s):
        for copy in sum_one_copies(s):
            copy.wait()
        own = R.gw[s, chunk(f, PART, 32), :].astype(F32)
        for d in range(3):
            own = own + R.r1[s, d].astype(F32)
        R.p1[s] = own
        sem = R.ar2_sem

        def one(d, carry):
            o = coarse_at(d)

            @pl.when(o < OWNERS)
            def _():
                remote(
                    R.p1.at[s, chunk(o, 8), :], R.r2.at[s, chunk(c, 8), :], sem.at[s, 0], sem.at[s, 1], (f, o)
                ).start()

            return carry

        lax.fori_loop(1, N_COARSE, one, 0)

    def sum_three(s):
        sem, sem3 = R.ar2_sem, R.ar3_sem

        @pl.when(c < OWNERS)
        def _():
            mine = chunk(c, 8)
            R.r2[s, mine, :] = R.p1[s, mine, :]
            wait_for(R.p1.at[s, pl.ds(0, (OWNERS - 1) * 8), :], sem.at[s, 0])
            wait_for(R.r2.at[s, pl.ds(0, (N_COARSE - 1) * 8), :], sem.at[s, 1])
            parts = [R.r2[s, j * 8 : j * 8 + 8, :] for j in range(N_COARSE)]
            while len(parts) > 1:
                parts = [parts[j] + parts[j + 1] for j in range(0, len(parts), 2)]
            R.r3[s, mine, :] = parts[0]

            def one(d, carry):
                remote(
                    R.r3.at[s, mine, :], R.r3.at[s, mine, :], sem3.at[s, 0], sem3.at[s, 1], (f, coarse_at(d))
                ).start()
                return carry

            lax.fori_loop(1, N_COARSE, one, 0)

        @pl.when(c >= OWNERS)
        def _():
            wait_for(R.p1.at[s], sem.at[s, 0])

    def sum_four_copies(s):
        mine = chunk(f, PART, 32)
        out = []
        for d in range(1, N_FINE):
            out.append(
                remote(
                    R.r3.at[s],
                    R.r4.at[s, mine, :],
                    R.ar4_sem.at[s, 0, d - 1],
                    R.ar4_sem.at[s, 1, d - 1],
                    (fine_at(d), c),
                )
            )
        return out

    def sum_four(s):
        sem = R.ar3_sem

        @pl.when(c < OWNERS)
        def _():
            wait_for(R.r2.at[s, pl.ds(0, (N_COARSE - 1) * 8), :], sem.at[s, 0])
            wait_for(R.r3.at[s, pl.ds(0, (OWNERS - 1) * 8), :], sem.at[s, 1])

        @pl.when(c >= OWNERS)
        def _():
            wait_for(R.r3.at[s], sem.at[s, 1])

        for copy in sum_four_copies(s):
            copy.start()
        R.r4[s, chunk(f, PART, 32), :] = R.r3[s]

    def sum_end(s):
        for copy in sum_four_copies(s):
            copy.wait()
        out, l = (O.fg, s) if s < 2 else (O.cg, s - 2)
        out.ei[l] = R.r4[s, 0:384, :]
        out.eo[l] = R.r4[s, 384:512, :]
        out.ni[l] = R.r4[s, 512:768, :]
        out.no[l] = R.r4[s, 768:896, :]

    fine = SimpleNamespace(
        n=NF, used=NF + HALO, tab=NF + HALO, own=NF, e=EF, tile=1024, block=512, S=R.f, W=I.fw, first=0, masked=False
    )
    coarse = SimpleNamespace(
        n=NC, used=3 * NC, tab=512, own=256, e=EC, tile=EC, block=NC, S=R.c, W=I.cw, first=2, masked=True
    )

    def project_own(v, l):
        w, h = v.W.ei, v.S.layers[l].tab[0 : v.n, :]
        into = v.S.proj if v.masked else v.S.wide
        into[0 : v.n, :] = dot(h, w[l, 128:256, :]).astype(into.dtype)
        into[v.tab : v.tab + v.n, :] = dot(h, w[l, 256:384, :]).astype(into.dtype)

    def project_rest(v, l):
        rest = v.S.layers[l].tab[v.n : v.tab, :]
        into = v.S.proj if v.masked else v.S.wide
        into[v.n : v.tab, :] = dot(rest, v.W.ei[l, 128:256, :]).astype(into.dtype)

    def forward(v, l, edges):
        S, W, A = v.S, v.W, v.S.layers[l]
        if not v.masked:
            scale = scale_for(column_peak(S.wide[...]))
            S.proj8[...] = halves(S.wide[...], scale)

        def one(i, peak):
            rows = chunk(i, v.tile)
            old = edges[rows, :]
            columns = ((S.cs[rows, :], 0, v.tab), (S.cr[rows, :], v.tab, v.own))
            if v.masked:
                z = gather_rows(columns, S.proj)
            else:
                z = joined(gather_rows(columns, S.proj8), scale)
            z = z + dot(old, W.ei[l, 0:128, :])
            gate = jax.nn.sigmoid(z)
            hidden = z * gate
            A.slope[rows, :] = gate * (1.0 + z - hidden)
            hidden = hidden.astype(BF)
            A.hid[rows, :] = hidden
            values, spread_by = normed(dot(hidden, W.eo[l]))
            A.n[rows, :] = values
            A.scale[rows, :] = jnp.broadcast_to(spread_by, values.shape)
            new = (old.astype(F32) + values).astype(BF)
            A.e[rows, :] = new
            return jnp.maximum(peak, column_peak(new.astype(F32)))

        peak = lax.fori_loop(0, v.e // v.tile, one, jnp.zeros((1, L), F32))
        if not v.masked:
            scale = scale_for(peak)

            def split(i, carry):
                rows = chunk(i, v.tile)
                S.e8[rows, :] = halves(A.e[rows, :].astype(F32), scale)
                return carry

            lax.fori_loop(0, v.e // v.tile, split, 0)

        def two(i, carry):
            rows = chunk(i, v.block)
            if v.masked:
                g = scatter_rows(S.rr, A.e, i * v.block, v.block, v.e)
            else:
                g = joined(scatter_rows(S.rr, S.e8, i * v.block, v.block, v.e), scale)
            A.g[rows, :] = g.astype(BF)
            return carry

        lax.fori_loop(0, v.n // v.block, two, 0)
        h = A.tab[0 : v.n, :]
        z = dot(h, W.ni[l, 0:128, :]) + dot(A.g[...], W.ni[l, 128:256, :])
        gate = jax.nn.sigmoid(z)
        hidden = z * gate
        A.slope2[...] = gate * (1.0 + z - hidden)
        hidden = hidden.astype(BF)
        A.hid2[...] = hidden
        values, spread_by = normed(dot(hidden, W.no[l]))
        A.n2[...] = values
        A.scale2[...] = jnp.broadcast_to(spread_by, values.shape)
        new = h.astype(F32) + values
        if v.masked:
            new = new * R.live[...]
        return new.astype(BF)

    def backward(v, l, edges, grad, edge_grad, send_rest, keep_edge, weights_done):
        S, W, A = v.S, v.W, v.S.layers[l]
        s, acc, gw = v.first + l, v.S.acc, R.gw
        dn = grad.astype(F32)
        if v.masked:
            dn = dn * R.live[...]
        dy = normed_back(dn, A.n2[...], A.scale2[...]).astype(BF)
        dz = (dot_nt(dy, W.no[l]) * A.slope2[...]).astype(BF)
        h = A.tab[0 : v.n, :]
        dg = dot_nt(dz, W.ni[l, 128:256, :])
        if v.masked:
            S.dg[0 : v.n, :] = dg.astype(BF)
        else:
            dg_scale = scale_for(column_peak(dg))
            S.dg8[...] = halves(dg, dg_scale)
        acc[...] = dn + dot_nt(dz, W.ni[l, 0:128, :])
        gw[s, 512:640, :] = dot_tn(h, dz).astype(BF)
        gw[s, 640:768, :] = dot_tn(A.g[...], dz).astype(BF)
        gw[s, 768:896, :] = dot_tn(A.hid2[...], dy).astype(BF)
        R.acc_b[...] = jnp.zeros((L, L), F32)
        R.acc_e[...] = jnp.zeros((L, L), F32)

        def one(i, peak):
            rows = chunk(i, v.tile)
            columns = ((S.cr[rows, :], 0, v.own),)
            if v.masked:
                dn = gather_rows(columns, S.dg)
            else:
                dn = joined(gather_rows(columns, S.dg8), dg_scale)
            if edge_grad is not None:
                dn = dn + edge_grad[rows, :].astype(F32)
            dy = normed_back(dn, A.n[rows, :], A.scale[rows, :]).astype(BF)
            dz = (dot_nt(dy, W.eo[l]) * A.slope[rows, :]).astype(BF)
            S.dz[rows, :] = dz
            R.acc_b[...] += dot_tn(A.hid[rows, :], dy)
            R.acc_e[...] += dot_tn(edges[rows, :], dz)
            if keep_edge:
                S.de[rows, :] = (dn + dot_nt(dz, W.ei[l, 0:128, :])).astype(BF)
            return jnp.maximum(peak, column_peak(dz.astype(F32)))

        peak = lax.fori_loop(0, v.e // v.tile, one, jnp.zeros((1, L), F32))
        if v.masked:

            def spread_back(rows_ref, first, count):
                return scatter_rows(rows_ref, S.dz, first, count, v.e).astype(BF)

        else:
            scale = scale_for(peak)

            def split(i, carry):
                rows = chunk(i, v.tile)
                S.e8[rows, :] = halves(S.dz[rows, :].astype(F32), scale)
                return carry

            lax.fori_loop(0, v.e // v.tile, split, 0)

            def spread_back(rows_ref, first, count):
                return joined(scatter_rows(rows_ref, S.e8, first, count, v.e), scale).astype(BF)

        rest = spread_back(S.rs, v.n, v.used - v.n)
        send_rest(dot_nt(rest, W.ei[l, 128:256, :]).astype(BF))
        gw[s, 0:128, :] = R.acc_e[...].astype(BF)
        gw[s, 384:512, :] = R.acc_b[...].astype(BF)
        R.acc_b[...] = dot_tn(A.tab[v.n : v.used, :], rest)
        R.acc_e[...] = jnp.zeros((L, L), F32)

        def two(i, carry):
            rows = chunk(i, v.block)
            h = A.tab[rows, :]
            part = spread_back(S.rs, i * v.block, v.block)
            R.acc_b[...] += dot_tn(h, part)
            other = spread_back(S.rr, i * v.block, v.block)
            R.acc_e[...] += dot_tn(h, other)
            acc[rows, :] += dot_nt(part, W.ei[l, 128:256, :]) + dot_nt(other, W.ei[l, 256:384, :])
            return carry

        lax.fori_loop(0, v.n // v.block, two, 0)
        gw[s, 128:256, :] = R.acc_b[...].astype(BF)
        gw[s, 256:384, :] = R.acc_e[...].astype(BF)
        weights_done(s)

    def place_column():
        return R.place[0][...]

    def place_wide():
        return jnp.broadcast_to(R.place[1][0:1, :], (WIDE, L))

    def pool_hot():
        return ones_where((iota((BLOCKS, NF), 1) >> 4) == iota((BLOCKS, NF), 0))

    def grow_hot():
        return ones_where((iota((NF, L), 0) >> 4) == iota((NF, L), 1))[:, 0:BLOCKS]

    def put_hot():
        return ones_where(iota((WIDE, L), 0) == place_wide())[:, 0:BLOCKS]

    def flag_hot():
        wide = place_wide()
        return ones_where((iota((WIDE, L), 0) == wide + CAP) & (wide >= 0))[:, 0:BLOCKS]

    def take_hot():
        return ones_where(jnp.concatenate([place_column()] * 4, axis=1) == iota((BLOCKS, WIDE), 1))

    def slot_of(index, offset):
        within = (index & (PAD - 1)) - offset
        return jnp.where((within >= 0) & (within < CAP), (index >> 4) * CAP + within, -1)

    def narrow_hot(offset):
        return ones_where(slot_of(iota((NC, WIDE), 1), offset) == iota((NC, WIDE), 0))

    def widen_hot():
        return ones_where(slot_of(iota((WIDE, 256), 0), 0) == iota((WIDE, 256), 1))[:, 0:NC]

    def halo_pick(tab, k):
        def one(j, carry):
            rows = chunk(j, L)
            R.hs[k][rows, :] = gather_rows(((R.halo_col[rows, :], 0, NF),), tab).astype(BF)
            return carry

        lax.fori_loop(0, N_FINE, one, 0)

    def halo_back(k):
        def send(values):
            R.hs[k][...] = values
            halo_start(R.hs[k], R.hr[k - 2], 0, R.hs_sem[k])

        return send

    def halo_add(k):
        halo_wait(R.hs[k], R.hr[k - 2], 0, R.hs_sem[k])

        def one(i, carry):
            rows = chunk(i, 512)
            R.f.acc[rows, :] += scatter_rows(R.halo_row, R.hr[k - 2], i * 512, 512, HALO)
            return carry

        lax.fori_loop(0, NF // 512, one, 0)

    def near_table(l):
        tab = R.c.layers[l].tab
        own = tab.at[pl.ds(0, NC), :]
        return near_copies(own, tab.at[pl.ds(NC, NC), :], own, tab.at[pl.ds(2 * NC, NC), :], R.near_sem[l])

    def near_grad(l):
        src, dst = R.ns[l], R.nr[l]
        low, high = pl.ds(0, NC), pl.ds(NC, NC)
        return near_copies(src.at[high, :], dst.at[low, :], src.at[low, :], dst.at[high, :], R.near_sem[2 + l])

    def start(copies):
        for copy in copies:
            copy.start()

    def wait(copies):
        for copy in copies:
            copy.wait()

    def enter():
        greet()
        spread(I.halo, R.halo_col, R.halo_row, HALO // L)
        halo_pick(I.node, 0)
        pl.semaphore_wait(barrier, N_FINE - 1 + N_COARSE - 1)
        halo_start(R.hs[0], R.f.layers[0].tab, NF, R.hs_sem[0])

    def prepare():
        R.f.layers[0].tab[0:NF, :] = I.node[...]
        project_own(fine, 0)
        spread(I.src, R.f.cs, R.f.rs, EF // L)
        spread(I.dst, R.f.cr, R.f.rr, EF // L)
        spread(I.csrc, R.c.cs, R.c.rs, EC // L)
        spread(I.cdst, R.c.cr, R.c.rr, EC // L)
        for l in (0, 1):
            R.c.layers[l].tab[3 * NC : 512, :] = jnp.zeros((512 - 3 * NC, L), BF)
        R.c.proj[512 + NC : 768, :] = jnp.zeros((256 - NC, L), BF)
        R.c.dg[NC:256, :] = jnp.zeros((256 - NC, L), BF)
        owner = jnp.broadcast_to(I.owner[...], (BLOCKS, L))
        below = jnp.full((L - BLOCKS, L), -1, I32)
        square = jnp.concatenate([owner, below], axis=0).T
        same = (owner == square[0:BLOCKS, :]) & (iota((BLOCKS, L), 1) < iota((BLOCKS, L), 0))
        rank = lane_sum(jnp.where(same, 1.0, 0.0)).astype(I32)
        place = owner * PAD + rank
        R.place[0][...] = place
        R.place[1][...] = jnp.concatenate([place, below], axis=0).T

    def fine_zero():
        halo_wait(R.hs[0], R.f.layers[0].tab, NF, R.hs_sem[0])
        project_rest(fine, 0)
        R.state_one[...] = forward(fine, 0, I.edge)

    def sink():
        pooled = (dot(pool_hot(), R.state_one[...]) * (1.0 / POOL)).astype(BF)
        flags = dot(flag_hot(), jnp.ones((BLOCKS, L), BF))
        R.ws[0][...] = (dot(put_hot(), pooled) + flags).astype(BF)
        wide_start(0)
        wide_wait(0)
        arrived = R.wr[0][...]
        R.live[...] = dot(narrow_hot(CAP), arrived)
        R.c.layers[0].tab[0:NC, :] = dot(narrow_hot(0), arrived).astype(BF)

    def coarse_layer(l):
        def run():
            start(near_table(l))
            project_own(coarse, l)
            wait(near_table(l))
            project_rest(coarse, l)
            new = forward(coarse, l, I.cedge if l == 0 else R.c.layers[0].e)
            if l == 0:
                R.c.layers[1].tab[0:NC, :] = new
            else:
                R.ws[1][...] = dot(widen_hot(), new).astype(BF)
                wide_start(1)

        return run

    def rise():
        wide_wait(1)
        picked = dot(take_hot(), R.wr[1][...]).astype(BF)
        R.f.layers[1].tab[0:NF, :] = (R.state_one[...].astype(F32) + dot(grow_hot(), picked)).astype(BF)
        halo_pick(R.f.layers[1].tab, 1)
        halo_start(R.hs[1], R.f.layers[1].tab, NF, R.hs_sem[1])
        project_own(fine, 1)
        halo_wait(R.hs[1], R.f.layers[1].tab, NF, R.hs_sem[1])
        project_rest(fine, 1)

    def fine_one():
        O.new_state[...] = forward(fine, 1, R.f.layers[0].e)

    def fine_one_back():
        backward(fine, 1, R.f.layers[0].e, I.cot[...], None, halo_back(2), True, sum_one)

    def sink_back():
        halo_add(2)
        grad_two = R.f.acc[...].astype(BF)
        R.grad_two[...] = grad_two
        R.ws[2][...] = dot(put_hot(), dot(pool_hot(), grad_two).astype(BF)).astype(BF)
        wide_start(2)
        sum_two(1)
        wide_wait(2)
        R.grad_c[...] = dot(narrow_hot(0), R.wr[2][...]).astype(BF)

    def coarse_back(l):
        def run():
            def send(values):
                R.ns[l][...] = values
                start(near_grad(l))

            edges, edge_grad = (I.cedge, R.c.de) if l == 0 else (R.c.layers[0].e, None)
            backward(coarse, l, edges, R.grad_c[...], edge_grad, send, l == 1, sum_one)
            if l == 1:
                sum_three(1)
            else:
                sum_two(3)
            wait(near_grad(l))
            dst = R.nr[l]
            total = R.c.acc[...] + dst[0:NC, :].astype(F32) + dst[NC : 2 * NC, :].astype(F32)
            R.grad_c[...] = total.astype(BF)

        return run

    def rise_back():
        R.ws[3][...] = dot(widen_hot(), R.grad_c[...]).astype(BF)
        wide_start(3)
        sum_four(1)
        sum_two(2)
        wide_wait(3)
        sunk = (dot(take_hot(), R.wr[3][...]) * (1.0 / POOL)).astype(BF)
        R.grad_one[...] = (R.grad_two[...].astype(F32) + dot(grow_hot(), sunk)).astype(BF)
        sum_three(3)

    def fine_zero_back():
        def weights_done(s):
            sum_three(2)
            sum_one(0)

        backward(fine, 0, I.edge, R.grad_one[...], R.f.de, halo_back(3), False, weights_done)

    def leave():
        sum_four(3)
        halo_add(3)
        sum_two(0)
        O.state_grad[...] = R.f.acc[...].astype(BF)
        sum_four(2)
        sum_end(1)
        sum_three(0)
        sum_end(3)
        sum_end(2)
        sum_four(0)
        sum_end(0)

    steps = (
        enter, prepare, fine_zero, sink, coarse_layer(0), coarse_layer(1), rise, fine_one, fine_one_back, sink_back,
        coarse_back(1), coarse_back(0), rise_back, fine_zero_back, leave,
    )
    for step in steps[:STEPS]:
        step()


def body(*arrays):
    arrays = list(arrays)
    for i, rows in ((3, EF // L), (4, EF // L), (7, EC // L), (8, EC // L)):
        arrays[i] = arrays[i].reshape(rows, L)
    outs = [jax.ShapeDtypeStruct((NF, L), BF)] * 2
    for _ in range(2):
        outs += [jax.ShapeDtypeStruct((2, rows, L), F32) for rows in (384, 128, 256, 128)]
    vm = pl.BlockSpec(memory_space=pltpu.VMEM)
    return pl.pallas_call(
        kernel,
        out_shape=tuple(outs),
        in_specs=[vm] * len(arrays),
        out_specs=tuple([vm] * len(outs)),
        scratch_shapes=flat(shapes()),
        compiler_params=pltpu.CompilerParams(
            collective_id=0, has_side_effects=True, vmem_limit_bytes=60 * 2**20
        ),
        cost_estimate=pl.CostEstimate(flops=40 * 10**9, bytes_accessed=8 * 2**20, transcendentals=4 * 10**6),
    )(*arrays)


def solution(mesh):
    rows = P(("fine", "coarse"), None)
    flat = P(("fine", "coarse"))
    placed = (rows, rows, rows, flat, flat, rows, rows, flat, flat, rows) + (P(),) * 8
    return jax.shard_map(
        body, mesh=mesh, in_specs=placed, out_specs=(rows, rows) + (P(),) * 8, check_vma=False
    )
```

time: 662 us -> 166 us (0.25); the launches traced: 652 us -> 165 us
  other arithmetic: 218 us -> 0 us
  Pallas kernels: 0 us -> 153 us
  local copies, waits for them, and re-layouts: 160 us -> 11.5 us
  waiting for transfers between devices: 135 us -> 0 us
  starting transfers between devices: 80.2 us -> 0 us
  matrix products: 41.8 us -> 0 us
  between operations: 17.1 us -> 0.68 us
    scatter-add x14 -> x0, other arithmetic: 182 us -> none  [the longest x8 117 us: graph_layer(): joined = jnp.concatenate([edges, table[senders], state[receivers]], axis=1)]
    pallas_call x0 -> x1, Pallas kernels: none -> 153 us  [body(): pl.pallas_call(kernel, out_shape=tuple(outs), in_specs=[vm] * len(arrays)...]
    gather x22 -> x0, local copies, waits for them, and re-layouts: 112 us -> none  [the longest x12 66.9 us: graph_layer(): joined = jnp.concatenate([edges, table[senders], state[receivers]], axis=1)]
    psum x1 -> x0, waiting for transfers between devices: 88.4 us -> none  [body(): lax.psum((g_fei, g_feo, g_fni, g_fno, g_cei, g_ceo, g_cni, g_cno), ('fine...]
    all_to_all x9 -> x0, starting transfers between devices: 62 us -> none  [the longest x4 36 us: fine_rows(): lax.all_to_all(values, 'fine', split_axis=0, concat_axis=0, tiled=True)]
    dot_general x52 -> x0, matrix products: 41.8 us -> none  [the longest x24 23.3 us: perceptron(): jnp.dot(hidden, w_second, preferred_element_type=jnp.float32)]
    all_to_all x9 -> x0, waiting for transfers between devices: 33.1 us -> none  [the longest x3 24 us: coarse_rows(): lax.all_to_all(values, 'coarse', split_axis=0, concat_axis=0, tiled=True)]
    unnamed x338 -> x31, local copies, waits for them, and re-layouts: 31.9 us -> 11.5 us
  transfers between devices with their start and end apart: 18 -> 0, of which waited for: 9 -> 0; matrix products, arithmetic and copies ran while one was open for 22% -> 0% of each run, Pallas kernels for 0% -> 0%
where the time goes in v1:
time: 166 us; the launch traced here: 165 us
  Pallas kernels  153 us (92%)
  local copies, waits for them, and re-layouts  11.5 us (7%)
    pallas_call x1, Pallas kernels, body(): pl.pallas_call(kernel, out_shape=tuple(outs), in_specs=[vm] * len(arrays)...  153 us
    unnamed x31, local copies, waits for them, and re-layouts  11.5 us

profile of v1, /device:TPU:1, one launch (start us, length us, event | category | flops | bytes accessed | tf_op | source)
XLA Modules:
  0.0 165.2 jit_solution(13160924101379915466)
XLA Ops:
  0.6 0.0 copy-start.9
  0.7 0.6 copy-done.9
  1.3 0.7 copy.28.args_6_
  2.0 153.0 %shard_map.249 = (bf16[1024,128]{1,0:T(8,128)(2,1)}, bf16[1024,128]{1,0:T(8,128)(2,1)}, f32[2,384,128]{2,1,0:T(8,128)}, f32[2,128,128]{2,1,0:T(8,128)}, f32[2,25...) custom-call(bf16[1024,128]{1,0:T(8,128)(2,1)} %args_0_.4, ...), custom_call_target="tpu_custom_call" | custom-call | flops 40000000000 | bytes 8388608 | tf_op jit(solution)/shard_map/pallas_call | solution.py:813
  155.1 0.0 copy-start.4
  155.1 1.7 %copy.39 = bf16[1024,128]{1,0:T(8,128)(2,1)} copy(bf16[1024,128]{1,0:T(8,128)(2,1)} %get-tuple-element.20) | data formatting | bytes 524288
  156.8 0.0 copy-done.4
  156.8 0.7 copy.40
  157.5 0.4 copy-done.1
  157.9 0.7 copy.41
  158.6 0.3 copy-done.8
  158.9 0.7 copy.42
  159.6 0.3 copy-done.3
  159.9 0.7 copy.43
  160.6 0.3 copy-done.7
  160.9 0.7 copy.44
  161.5 0.0 copy-done
  161.6 0.7 copy.45
  162.3 0.3 copy-done.6
  162.6 0.7 copy.46
  163.2 0.3 copy-done.2
  163.6 0.7 copy.47
  164.3 0.3 copy-done.5
  164.6 0.7 copy.48
  (8 shorter events, 0.0 us)
Async XLA Ops:
  0.6 0.7 copy-start.9
  155.1 1.7 %copy-start.4 = (bf16[1024,128]{1,0:T(8,128)(2,1)S(1)}, bf16[1024,128]{1,0:T(8,128)(2,1)}, u32[]{:S(2)}) copy-start(bf16[1024,128]{1,0:T(8,128)(2,1)} %get-tuple-element.21) | copy-start | bytes 786436
  156.8 1.1 copy-start.1
  157.9 1.0 copy-start.8
  158.9 1.0 copy-start.3
  159.9 1.0 copy-start.7
  159.9 1.7 %copy-start = (f32[2,384,128]{2,1,0:T(8,128)S(1)}, f32[2,384,128]{2,1,0:T(8,128)}, u32[]{:S(2)}) copy-start(f32[2,384,128]{2,1,0:T(8,128)} %get-tuple-element.26) | copy-start | bytes 1179652
  161.6 1.0 copy-start.6
  162.6 1.0 copy-start.2
  163.6 1.0 copy-start.5

commit v2 on v1

--- a/solution.py
+++ b/solution.py
@@ -22,8 +22,8 @@
 N_FINE, N_COARSE = 4, 32
 WIDE = N_COARSE * PAD
 SET = 896
-PART = SET // N_FINE
-OWNERS = PART // 8
+LATE = 256
+OWNED = 32
 EPS = 1e-05
 
 
@@ -174,21 +174,23 @@
         hr=[vm(HALO, L, dtype=BF) for _ in range(2)],
         ws=[vm(WIDE, L, dtype=BF) for _ in range(4)],
         wr=[vm(WIDE, L, dtype=BF) for _ in range(4)],
-        ns=[vm(2 * NC, L, dtype=BF) for _ in range(2)],
-        nr=[vm(2 * NC, L, dtype=BF) for _ in range(2)],
+        ns=vm(2 * NC, L, dtype=BF),
+        nr=vm(2 * NC, L, dtype=BF),
+        parts=vm(512, L, dtype=BF),
         gw=vm(4, SET, L, dtype=BF),
-        r1=vm(4, 3, PART, L, dtype=BF),
-        p1=vm(4, PART, L),
-        r2=vm(4, N_COARSE * 8, L),
-        r3=vm(4, PART, L),
-        r4=vm(4, SET, L),
+        late=vm(LATE, L),
+        late_got=vm(LATE, L),
+        late_quad=vm(N_FINE, 8, L),
+        late_sum=vm(LATE, L),
+        got=vm(4, N_COARSE * OWNED, L, dtype=BF),
+        quad=vm(4, N_FINE, OWNED, L),
+        sums=vm(4, N_COARSE * OWNED, L),
+        one_sem=dma((5, 2)),
+        two_sem=dma((5, 2, 3)),
+        three_sem=dma((5, 2)),
         hs_sem=[dma((2, 3)) for _ in range(4)],
         ws_sem=[dma((2,)) for _ in range(4)],
-        near_sem=[dma((2, 2)) for _ in range(4)],
-        ar1_sem=dma((4, 2, 3)),
-        ar2_sem=dma((4, 2)),
-        ar3_sem=dma((4, 2)),
-        ar4_sem=dma((4, 2, 3)),
+        near_sem=[dma((2, 2)) for _ in range(2)],
     )
 
 
@@ -216,7 +218,7 @@
         node=None, edge=None, cedge=None, src=None, dst=None, halo=None, owner=None, csrc=None, cdst=None, cot=None,
         fw=weights(), cw=weights(),
     )
-    outputs = SimpleNamespace(new_state=None, state_grad=None, fg=weights(), cg=weights())
+    outputs = SimpleNamespace(new_state=None, state_grad=None, sums=None)
     return inputs, outputs
 
 
@@ -304,12 +306,13 @@
             remote(src.at[chunk(o, PAD), :], dst.at[chunk(c, PAD), :], sem.at[0], sem.at[1], (f, o)).start()
             return carry
 
-        lax.fori_loop(1, N_COARSE, one, 0)
+        lax.fori_loop(N_COARSE // 2, N_COARSE, one, 0)
+        lax.fori_loop(1, N_COARSE // 2, one, 0)
         dst[chunk(c, PAD), :] = src[chunk(c, PAD), :]
 
     def wide_wait(k):
-        src, dst, sem = R.ws[k], R.wr[k], R.ws_sem[k]
-        wait_for(src.at[pl.ds(0, WIDE - PAD), :], sem.at[0])
+        dst, sem = R.wr[k], R.ws_sem[k]
+        wait_for(dst.at[pl.ds(0, WIDE - PAD), :], sem.at[0])
         wait_for(dst.at[pl.ds(0, WIDE - PAD), :], sem.at[1])
 
     def near_copies(up_src, up_dst, down_src, down_dst, sem):
@@ -318,112 +321,93 @@
             remote(down_src, down_dst, sem.at[0, 1], sem.at[1, 1], (f, coarse_at(-1))),
         )
 
-    def sum_one_copies(s):
-        out = []
-        for d in range(1, N_FINE):
-            q = fine_at(d)
-            out.append(
-                remote(
-                    R.gw.at[s, chunk(q, PART, 32), :],
-                    R.r1.at[s, d - 1],
-                    R.ar1_sem.at[s, 0, d - 1],
-                    R.ar1_sem.at[s, 1, d - 1],
-                    (q, c),
-                )
-            )
-        return out
-
-    def sum_one(s):
-        for copy in sum_one_copies(s):
-            copy.start()
-
-    def sum_two(s):
-        for copy in sum_one_copies(s):
-            copy.wait()
-        own = R.gw[s, chunk(f, PART, 32), :].astype(F32)
-        for d in range(3):
-            own = own + R.r1[s, d].astype(F32)
-        R.p1[s] = own
-        sem = R.ar2_sem
-
-        def one(d, carry):
-            o = coarse_at(d)
-
-            @pl.when(o < OWNERS)
-            def _():
-                remote(
-                    R.p1.at[s, chunk(o, 8), :], R.r2.at[s, chunk(c, 8), :], sem.at[s, 0], sem.at[s, 1], (f, o)
-                ).start()
-
-            return carry
-
-        lax.fori_loop(1, N_COARSE, one, 0)
-
-    def sum_three(s):
-        sem, sem3 = R.ar2_sem, R.ar3_sem
-
-        @pl.when(c < OWNERS)
-        def _():
-            mine = chunk(c, 8)
-            R.r2[s, mine, :] = R.p1[s, mine, :]
-            wait_for(R.p1.at[s, pl.ds(0, (OWNERS - 1) * 8), :], sem.at[s, 0])
-            wait_for(R.r2.at[s, pl.ds(0, (N_COARSE - 1) * 8), :], sem.at[s, 1])
-            parts = [R.r2[s, j * 8 : j * 8 + 8, :] for j in range(N_COARSE)]
-            while len(parts) > 1:
-                parts = [parts[j] + parts[j + 1] for j in range(0, len(parts), 2)]
-            R.r3[s, mine, :] = parts[0]
-
-            def one(d, carry):
-                remote(
-                    R.r3.at[s, mine, :], R.r3.at[s, mine, :], sem3.at[s, 0], sem3.at[s, 1], (f, coarse_at(d))
-                ).start()
+    def summing(k, owners, block, src, got, quad, dst):
+        sem, group_sem, last_sem = R.one_sem.at[k], R.two_sem.at[k], R.three_sem.at[k]
+        mine = chunk(c, block)
+
+        def owner(run):
+            run() if owners == N_COARSE else pl.when(c < owners)(run)
+
+        def other(run):
+            if owners < N_COARSE:
+                pl.when(c >= owners)(run)
+
+        def group():
+            return [
+                remote(quad.at[f], quad.at[f], group_sem.at[0, d - 1], group_sem.at[1, d - 1], (fine_at(d), c))
+                for d in range(1, N_FINE)
+            ]
+
+        def one():
+            def send(d, carry):
+                o = coarse_at(d)
+
+                def go():
+                    remote(src.at[chunk(o, block), :], got.at[mine, :], sem.at[0], sem.at[1], (f, o)).start()
+
+                go() if owners == N_COARSE else pl.when(o < owners)(go)
                 return carry
 
-            lax.fori_loop(1, N_COARSE, one, 0)
-
-        @pl.when(c >= OWNERS)
-        def _():
-            wait_for(R.p1.at[s], sem.at[s, 0])
-
-    def sum_four_copies(s):
-        mine = chunk(f, PART, 32)
-        out = []
-        for d in range(1, N_FINE):
-            out.append(
-                remote(
-                    R.r3.at[s],
-                    R.r4.at[s, mine, :],
-                    R.ar4_sem.at[s, 0, d - 1],
-                    R.ar4_sem.at[s, 1, d - 1],
-                    (fine_at(d), c),
-                )
-            )
-        return out
-
-    def sum_four(s):
-        sem = R.ar3_sem
-
-        @pl.when(c < OWNERS)
-        def _():
-            wait_for(R.r2.at[s, pl.ds(0, (N_COARSE - 1) * 8), :], sem.at[s, 0])
-            wait_for(R.r3.at[s, pl.ds(0, (OWNERS - 1) * 8), :], sem.at[s, 1])
-
-        @pl.when(c >= OWNERS)
-        def _():
-            wait_for(R.r3.at[s], sem.at[s, 1])
-
-        for copy in sum_four_copies(s):
-            copy.start()
-        R.r4[s, chunk(f, PART, 32), :] = R.r3[s]
-
-    def sum_end(s):
-        for copy in sum_four_copies(s):
-            copy.wait()
-        out, l = (O.fg, s) if s < 2 else (O.cg, s - 2)
-        out.ei[l] = R.r4[s, 0:384, :]
-        out.eo[l] = R.r4[s, 384:512, :]
-        out.ni[l] = R.r4[s, 512:768, :]
-        out.no[l] = R.r4[s, 768:896, :]
+            lax.fori_loop(N_COARSE // 2, N_COARSE, send, 0)
+            lax.fori_loop(1, N_COARSE // 2, send, 0)
+
+        def two():
+            def run():
+                got[mine, :] = src[mine, :]
+                wait_for(got.at[pl.ds(0, (owners - 1) * block), :], sem.at[0])
+                wait_for(got.at[pl.ds(0, (N_COARSE - 1) * block), :], sem.at[1])
+                parts = [got[j * block : (j + 1) * block, :].astype(F32) for j in range(N_COARSE)]
+                while len(parts) > 1:
+                    parts = [parts[j] + parts[j + 1] for j in range(0, len(parts), 2)]
+                quad[f] = parts[0]
+                for copy in group():
+                    copy.start()
+
+            owner(run)
+            other(lambda: wait_for(got.at[pl.ds(0, owners * block), :], sem.at[0]))
+
+        def three():
+            def run():
+                for copy in group():
+                    copy.wait()
+                dst[mine, :] = (quad[0] + quad[1]) + (quad[2] + quad[3])
+
+                def send(d, carry):
+                    o = coarse_at(d)
+                    remote(dst.at[mine, :], dst.at[mine, :], last_sem.at[0], last_sem.at[1], (f, o)).start()
+                    return carry
+
+                lax.fori_loop(N_COARSE // 2, N_COARSE, send, 0)
+                lax.fori_loop(1, N_COARSE // 2, send, 0)
+
+            owner(run)
+
+        def four():
+            def run():
+                wait_for(dst.at[pl.ds(0, (N_COARSE - 1) * block), :], last_sem.at[0])
+                wait_for(dst.at[pl.ds(0, (owners - 1) * block), :], last_sem.at[1])
+
+            owner(run)
+            other(lambda: wait_for(dst.at[pl.ds(0, owners * block), :], last_sem.at[1]))
+
+        return SimpleNamespace(one=one, two=two, three=three, four=four)
+
+    def summing_set(s):
+        first = LATE if s == 0 else 0
+        count = SET - first
+        work = summing(
+            s, count // OWNED, OWNED, R.gw.at[s, pl.ds(first, count), :], R.got.at[s], R.quad.at[s], R.sums.at[s]
+        )
+
+        def end():
+            work.four()
+            O.sums[s, first:SET, :] = R.sums[s, 0:count, :]
+
+        work.end = end
+        return work
+
+    total = [summing_set(s) for s in range(4)]
+    late = summing(4, N_COARSE, 8, R.late, R.late_got, R.late_quad, R.late_sum)
 
     fine = SimpleNamespace(
         n=NF, used=NF + HALO, tab=NF + HALO, own=NF, e=EF, tile=1024, block=512, S=R.f, W=I.fw, first=0, masked=False
@@ -506,7 +490,7 @@
             new = new * R.live[...]
         return new.astype(BF)
 
-    def backward(v, l, edges, grad, edge_grad, send_rest, keep_edge, weights_done):
+    def backward(v, l, edges, grad, edge_grad, send_rest, keep_edge, edges_done):
         S, W, A = v.S, v.W, v.S.layers[l]
         s, acc, gw = v.first + l, v.S.acc, R.gw
         dn = grad.astype(F32)
@@ -565,10 +549,11 @@
             def spread_back(rows_ref, first, count):
                 return joined(scatter_rows(rows_ref, S.e8, first, count, v.e), scale).astype(BF)
 
+        gw[s, 256:384, :] = R.acc_e[...].astype(BF)
+        gw[s, 384:512, :] = R.acc_b[...].astype(BF)
+        edges_done()
         rest = spread_back(S.rs, v.n, v.used - v.n)
         send_rest(dot_nt(rest, W.ei[l, 128:256, :]).astype(BF))
-        gw[s, 0:128, :] = R.acc_e[...].astype(BF)
-        gw[s, 384:512, :] = R.acc_b[...].astype(BF)
         R.acc_b[...] = dot_tn(A.tab[v.n : v.used, :], rest)
         R.acc_e[...] = jnp.zeros((L, L), F32)
 
@@ -583,9 +568,8 @@
             return carry
 
         lax.fori_loop(0, v.n // v.block, two, 0)
-        gw[s, 128:256, :] = R.acc_b[...].astype(BF)
-        gw[s, 256:384, :] = R.acc_e[...].astype(BF)
-        weights_done(s)
+        gw[s, 0:128, :] = R.acc_b[...].astype(BF)
+        gw[s, 128:256, :] = R.acc_e[...].astype(BF)
 
     def place_column():
         return R.place[0][...]
@@ -602,30 +586,69 @@
     def put_hot():
         return ones_where(iota((WIDE, L), 0) == place_wide())[:, 0:BLOCKS]
 
-    def flag_hot():
+    def three_places(owner, rank):
+        places = []
+        for part, shift in ((0, 0), (1, 1), (2, N_COARSE - 1)):
+            places.append(((owner + shift) & (N_COARSE - 1)) * PAD + part * CAP + rank)
+        return places
+
+    def put_three():
         wide = place_wide()
-        return ones_where((iota((WIDE, L), 0) == wide + CAP) & (wide >= 0))[:, 0:BLOCKS]
+        down = iota((WIDE, L), 0)
+        a, b, d = three_places(wide >> 4, wide & (PAD - 1))
+        return ones_where((down == a) | (down == b) | (down == d))[:, 0:BLOCKS]
+
+    def put_flags():
+        row = ones_where(iota((WIDE, L), 0) == (place_wide() | (PAD - 1)))[:, 0:BLOCKS]
+        lane = ones_where(iota((BLOCKS, L), 1) == (place_column() & (PAD - 1)))
+        return dot(row, lane)
 
     def take_hot():
         return ones_where(jnp.concatenate([place_column()] * 4, axis=1) == iota((BLOCKS, WIDE), 1))
 
-    def slot_of(index, offset):
-        within = (index & (PAD - 1)) - offset
-        return jnp.where((within >= 0) & (within < CAP), (index >> 4) * CAP + within, -1)
-
-    def narrow_hot(offset):
-        return ones_where(slot_of(iota((NC, WIDE), 1), offset) == iota((NC, WIDE), 0))
-
-    def widen_hot():
-        return ones_where(slot_of(iota((WIDE, 256), 0), 0) == iota((WIDE, 256), 1))[:, 0:NC]
+    def take_three():
+        place = place_column()
+        across = iota((BLOCKS, WIDE), 1)
+        a, b, d = (jnp.concatenate([at] * 4, axis=1) for at in three_places(place >> 4, place & (PAD - 1)))
+        return ones_where((across == a) | (across == b) | (across == d))
+
+    def slot_of(index):
+        within = index & (PAD - 1)
+        return jnp.where(within < CAP, (index >> 4) * CAP + within, -1)
+
+    def three_of(index):
+        within = index & (PAD - 1)
+        part = jnp.where(within >= 2 * CAP, 2, jnp.where(within >= CAP, 1, 0))
+        return jnp.where(within < 3 * CAP, part * (NC - CAP) + (index >> 4) * CAP + within, -1)
+
+    def across_hot(rows, places):
+        down = iota((rows, 128), 0).astype(I16)
+        parts = []
+        for k in range(0, WIDE, 128):
+            at = places(iota((16, 128), 1) + k).astype(I16)
+            parts.append(ones_where(down == jnp.concatenate([at] * (rows // 16), axis=0)))
+        return jnp.concatenate(parts, axis=1)
+
+    def apart_hot(places, width):
+        at = places(iota((WIDE, 128), 0)).astype(I16)
+        lanes = iota((16, 128), 1).astype(I16)
+        parts = []
+        for k in range(0, width, 128):
+            here = jnp.concatenate([lanes + jnp.asarray(k, I16)] * (WIDE // 16), axis=0)
+            parts.append(ones_where(at == here))
+        return jnp.concatenate(parts, axis=1)
+
+    def live_rows(arrived):
+        slot = iota((NC, WIDE), 0)
+        first = (iota((NC, WIDE), 1) >> 4) * CAP
+        last_row = (iota((NC, WIDE), 1) & (PAD - 1)) == PAD - 1
+        row = dot(ones_where(last_row & (slot >= first) & (slot < first + CAP)), arrived)
+        count = iota((NC, L), 0).astype(F32)
+        within = iota((NC, L), 0) - jnp.floor((count + 0.5) * (1.0 / CAP)).astype(I32) * CAP
+        return jnp.broadcast_to(lane_sum(jnp.where(iota((NC, L), 1) == within, row, 0.0)), (NC, L))
 
     def halo_pick(tab, k):
-        def one(j, carry):
-            rows = chunk(j, L)
-            R.hs[k][rows, :] = gather_rows(((R.halo_col[rows, :], 0, NF),), tab).astype(BF)
-            return carry
-
-        lax.fori_loop(0, N_FINE, one, 0)
+        R.hs[k][...] = gather_rows(((R.halo_col[...], 0, NF),), tab).astype(BF)
 
     def halo_back(k):
         def send(values):
@@ -644,15 +667,16 @@
 
         lax.fori_loop(0, NF // 512, one, 0)
 
-    def near_table(l):
-        tab = R.c.layers[l].tab
+    def near_table():
+        tab = R.c.layers[1].tab
         own = tab.at[pl.ds(0, NC), :]
-        return near_copies(own, tab.at[pl.ds(NC, NC), :], own, tab.at[pl.ds(2 * NC, NC), :], R.near_sem[l])
-
-    def near_grad(l):
-        src, dst = R.ns[l], R.nr[l]
+        return near_copies(own, tab.at[pl.ds(NC, NC), :], own, tab.at[pl.ds(2 * NC, NC), :], R.near_sem[0])
+
+    def near_grad():
         low, high = pl.ds(0, NC), pl.ds(NC, NC)
-        return near_copies(src.at[high, :], dst.at[low, :], src.at[low, :], dst.at[high, :], R.near_sem[2 + l])
+        return near_copies(
+            R.ns.at[high, :], R.nr.at[low, :], R.ns.at[low, :], R.nr.at[high, :], R.near_sem[1]
+        )
 
     def start(copies):
         for copy in copies:
@@ -661,23 +685,26 @@
     def wait(copies):
         for copy in copies:
             copy.wait()
+
+    def nothing():
+        pass
 
     def enter():
         greet()
         spread(I.halo, R.halo_col, R.halo_row, HALO // L)
         halo_pick(I.node, 0)
+        spread(I.src, R.f.cs, R.f.rs, EF // L)
+        spread(I.dst, R.f.cr, R.f.rr, EF // L)
         pl.semaphore_wait(barrier, N_FINE - 1 + N_COARSE - 1)
         halo_start(R.hs[0], R.f.layers[0].tab, NF, R.hs_sem[0])
 
     def prepare():
         R.f.layers[0].tab[0:NF, :] = I.node[...]
         project_own(fine, 0)
-        spread(I.src, R.f.cs, R.f.rs, EF // L)
-        spread(I.dst, R.f.cr, R.f.rr, EF // L)
         spread(I.csrc, R.c.cs, R.c.rs, EC // L)
         spread(I.cdst, R.c.cr, R.c.rr, EC // L)
-        for l in (0, 1):
-            R.c.layers[l].tab[3 * NC : 512, :] = jnp.zeros((512 - 3 * NC, L), BF)
+        R.c.layers[1].tab[3 * NC : 512, :] = jnp.zeros((512 - 3 * NC, L), BF)
+        R.parts[3 * NC : 512, :] = jnp.zeros((512 - 3 * NC, L), BF)
         R.c.proj[512 + NC : 768, :] = jnp.zeros((256 - NC, L), BF)
         R.c.dg[NC:256, :] = jnp.zeros((256 - NC, L), BF)
         owner = jnp.broadcast_to(I.owner[...], (BLOCKS, L))
@@ -696,25 +723,26 @@
 
     def sink():
         pooled = (dot(pool_hot(), R.state_one[...]) * (1.0 / POOL)).astype(BF)
-        flags = dot(flag_hot(), jnp.ones((BLOCKS, L), BF))
-        R.ws[0][...] = (dot(put_hot(), pooled) + flags).astype(BF)
+        R.ws[0][...] = (dot(put_three(), pooled) + put_flags()).astype(BF)
         wide_start(0)
         wide_wait(0)
         arrived = R.wr[0][...]
-        R.live[...] = dot(narrow_hot(CAP), arrived)
-        R.c.layers[0].tab[0:NC, :] = dot(narrow_hot(0), arrived).astype(BF)
+        R.c.layers[0].tab[...] = dot(across_hot(512, three_of), arrived).astype(BF)
+        R.live[...] = live_rows(arrived)
 
     def coarse_layer(l):
         def run():
-            start(near_table(l))
+            if l == 1:
+                start(near_table())
             project_own(coarse, l)
-            wait(near_table(l))
+            if l == 1:
+                wait(near_table())
             project_rest(coarse, l)
             new = forward(coarse, l, I.cedge if l == 0 else R.c.layers[0].e)
             if l == 0:
                 R.c.layers[1].tab[0:NC, :] = new
             else:
-                R.ws[1][...] = dot(widen_hot(), new).astype(BF)
+                R.ws[1][...] = dot(apart_hot(slot_of, 256)[:, 0:NC], new).astype(BF)
                 wide_start(1)
 
         return run
@@ -733,7 +761,7 @@
         O.new_state[...] = forward(fine, 1, R.f.layers[0].e)
 
     def fine_one_back():
-        backward(fine, 1, R.f.layers[0].e, I.cot[...], None, halo_back(2), True, sum_one)
+        backward(fine, 1, R.f.layers[0].e, I.cot[...], None, halo_back(2), True, nothing)
 
     def sink_back():
         halo_add(2)
@@ -741,58 +769,66 @@
         R.grad_two[...] = grad_two
         R.ws[2][...] = dot(put_hot(), dot(pool_hot(), grad_two).astype(BF)).astype(BF)
         wide_start(2)
-        sum_two(1)
+        total[1].one()
         wide_wait(2)
-        R.grad_c[...] = dot(narrow_hot(0), R.wr[2][...]).astype(BF)
+        R.grad_c[...] = dot(across_hot(NC, slot_of), R.wr[2][...]).astype(BF)
 
     def coarse_back(l):
         def run():
             def send(values):
-                R.ns[l][...] = values
-                start(near_grad(l))
+                if l == 1:
+                    R.ns[...] = values
+                    start(near_grad())
+                else:
+                    R.parts[NC : 3 * NC, :] = values
 
             edges, edge_grad = (I.cedge, R.c.de) if l == 0 else (R.c.layers[0].e, None)
-            backward(coarse, l, edges, R.grad_c[...], edge_grad, send, l == 1, sum_one)
+            backward(coarse, l, edges, R.grad_c[...], edge_grad, send, l == 1, nothing)
             if l == 1:
-                sum_three(1)
+                total[3].one()
+                total[1].two()
+                wait(near_grad())
+                grad = R.c.acc[...] + R.nr[0:NC, :].astype(F32) + R.nr[NC : 2 * NC, :].astype(F32)
+                R.grad_c[...] = grad.astype(BF)
             else:
-                sum_two(3)
-            wait(near_grad(l))
-            dst = R.nr[l]
-            total = R.c.acc[...] + dst[0:NC, :].astype(F32) + dst[NC : 2 * NC, :].astype(F32)
-            R.grad_c[...] = total.astype(BF)
+                R.parts[0:NC, :] = R.c.acc[...].astype(BF)
+                R.ws[3][...] = dot(apart_hot(three_of, 512), R.parts[...]).astype(BF)
+                wide_start(3)
 
         return run
 
     def rise_back():
-        R.ws[3][...] = dot(widen_hot(), R.grad_c[...]).astype(BF)
-        wide_start(3)
-        sum_four(1)
-        sum_two(2)
+        total[2].one()
+        total[1].three()
+        total[3].two()
         wide_wait(3)
-        sunk = (dot(take_hot(), R.wr[3][...]) * (1.0 / POOL)).astype(BF)
+        sunk = (dot(take_three(), R.wr[3][...]).astype(BF).astype(F32) * (1.0 / POOL)).astype(BF)
         R.grad_one[...] = (R.grad_two[...].astype(F32) + dot(grow_hot(), sunk)).astype(BF)
-        sum_three(3)
 
     def fine_zero_back():
-        def weights_done(s):
-            sum_three(2)
-            sum_one(0)
-
-        backward(fine, 0, I.edge, R.grad_one[...], R.f.de, halo_back(3), False, weights_done)
+        def edges_done():
+            total[0].one()
+            total[2].two()
+            total[3].three()
+
+        backward(fine, 0, I.edge, R.grad_one[...], R.f.de, halo_back(3), False, edges_done)
+        R.late[...] = R.gw[0, 0:LATE, :].astype(F32)
+        late.one()
 
     def leave():
-        sum_four(3)
+        total[0].two()
+        total[2].three()
         halo_add(3)
-        sum_two(0)
         O.state_grad[...] = R.f.acc[...].astype(BF)
-        sum_four(2)
-        sum_end(1)
-        sum_three(0)
-        sum_end(3)
-        sum_end(2)
-        sum_four(0)
-        sum_end(0)
+        late.two()
+        total[0].three()
+        total[1].end()
+        late.three()
+        total[3].end()
+        total[2].end()
+        total[0].end()
+        late.four()
+        O.sums[0, 0:LATE, :] = R.late_sum[...]
 
     steps = (
         enter, prepare, fine_zero, sink, coarse_layer(0), coarse_layer(1), rise, fine_one, fine_one_back, sink_back,
@@ -802,25 +838,51 @@
         step()
 
 
+def spread_out(state, grad, sums, *refs):
+    outs, sem = refs[:-1], refs[-1]
+    pairs = [(state, outs[0]), (grad, outs[1])]
+    for s in range(4):
+        ei, eo, ni, no = outs[2 + 4 * (s // 2) : 6 + 4 * (s // 2)]
+        l = s % 2
+        for out, there, here, rows in (
+            (ei, 0, 256, 128), (ei, 128, 0, 256), (eo, 0, 384, 128), (ni, 0, 512, 256), (no, 0, 768, 128)
+        ):
+            pairs.append((sums.at[s, pl.ds(here, rows), :], out.at[l, pl.ds(there, rows), :]))
+    copies = [pltpu.make_async_copy(src, dst, sem.at[k]) for k, (src, dst) in enumerate(pairs)]
+    for copy in copies:
+        copy.start()
+    for copy in copies:
+        copy.wait()
+
+
 def body(*arrays):
     arrays = list(arrays)
     for i, rows in ((3, EF // L), (4, EF // L), (7, EC // L), (8, EC // L)):
         arrays[i] = arrays[i].reshape(rows, L)
-    outs = [jax.ShapeDtypeStruct((NF, L), BF)] * 2
-    for _ in range(2):
-        outs += [jax.ShapeDtypeStruct((2, rows, L), F32) for rows in (384, 128, 256, 128)]
-    vm = pl.BlockSpec(memory_space=pltpu.VMEM)
-    return pl.pallas_call(
+    states = [jax.ShapeDtypeStruct((NF, L), BF)] * 2
+    vm_spec = pl.BlockSpec(memory_space=pltpu.VMEM)
+    any_spec = pl.BlockSpec(memory_space=pl.ANY)
+    results = pl.pallas_call(
         kernel,
-        out_shape=tuple(outs),
-        in_specs=[vm] * len(arrays),
-        out_specs=tuple([vm] * len(outs)),
+        out_shape=tuple(states + [jax.ShapeDtypeStruct((4, SET, L), F32)]),
+        in_specs=[vm_spec] * len(arrays),
+        out_specs=(vm_spec,) * 3,
         scratch_shapes=flat(shapes()),
         compiler_params=pltpu.CompilerParams(
             collective_id=0, has_side_effects=True, vmem_limit_bytes=60 * 2**20
         ),
         cost_estimate=pl.CostEstimate(flops=40 * 10**9, bytes_accessed=8 * 2**20, transcendentals=4 * 10**6),
     )(*arrays)
+    outs = list(states)
+    for _ in range(2):
+        outs += [jax.ShapeDtypeStruct((2, rows, L), F32) for rows in (384, 128, 256, 128)]
+    return pl.pallas_call(
+        spread_out,
+        out_shape=tuple(outs),
+        in_specs=[vm_spec] * 3,
+        out_specs=(any_spec,) * len(outs),
+        scratch_shapes=[pltpu.SemaphoreType.DMA((22,))],
+    )(*results)
 
 
 def solution(mesh):

time: 166 us -> 141 us (0.85)
  Pallas kernels: 153 us -> 138 us
  local copies, waits for them, and re-layouts: 11.5 us -> 1.36 us
    pallas_call x1 -> x2, Pallas kernels: 153 us -> 138 us  [the longest x1 135 us: body(): pl.pallas_call(kernel, out_shape=tuple(states + [jax.ShapeDtypeStruct((4,...]
    unnamed x31 -> x1, local copies, waits for them, and re-layouts: 11.5 us -> 1.36 us
where the time goes in v2:
time: 141 us
  Pallas kernels  138 us (98%)
    pallas_call x1, Pallas kernels, body(): pl.pallas_call(kernel, out_shape=tuple(states + [jax.ShapeDtypeStruct((4,...  135 us
    pallas_call x1, Pallas kernels, body(): pl.pallas_call(spread_out, out_shape=tuple(outs), in_specs=[vm_spec] * 3,...  3.25 us

profile of v2, /device:TPU:1, one launch (start us, length us, event | category | flops | bytes accessed | tf_op | source)
XLA Modules:
  0.0 140.7 jit_solution(9507131451520135785)
XLA Ops:
  0.6 1.4 copy.28.args_6_
  2.0 135.2 %shard_map.249 = (bf16[1024,128]{1,0:T(8,128)(2,1)}, bf16[1024,128]{1,0:T(8,128)(2,1)}, f32[4,896,128]{2,1,0:T(8,128)}) custom-call(bf16[1024,128]{1,0:T(8,128)(2,1)} %args_0_.4, bf16[4096,128]{1,0:T(8,128)(2,1)} %args_1_.4, bf16[640,128]{1,0:T(8,128)(2,1)} %args_2_.4, s32[32,128]{1,0:T(8,128)} %bitcast.4, s32[32,128]{1,0:T(8,128)} %bitcast.5, ...), custom_call_target="tpu_custom_call" | custom-call | flops 40000000000 | bytes 8388608 | tf_op jit(solution)/shard_map/pallas_call | solution.py:865
  137.2 3.2 %shard_map.250 = (bf16[1024,128]{1,0:T(8,128)(2,1)}, bf16[1024,128]{1,0:T(8,128)(2,1)}, f32[2,384,128]{2,1,0:T(8,128)}, f32[2,128,128]{2,1,0:T(8,128)}, f32[2,25...) custom-call(bf16[1024,128]{1,0:T(8,128)(2,1)} %get-tuple-element.13., ...), custom_call_target="tpu_custom_call" | custom-call | tf_op jit(solution)/shard_map/pallas_call | solution.py:879

commit v3 on v2

--- a/solution.py
+++ b/solution.py
@@ -74,10 +74,10 @@
 
 def gather_rows(columns, table):
     total = None
-    for column, base, width in columns:
+    for column, first, base, width in columns:
         for k in range(0, width, 256):
             size = min(256, width - k)
-            part = dot(hot_columns(column, k, size, table.dtype), table[base + k : base + k + size, :])
+            part = dot(hot_columns(column, first + k, size, table.dtype), table[base + k : base + k + size, :])
             total = part if total is None else total + part
     return total
 
@@ -150,6 +150,11 @@
         dg8=vm(own, 2 * L, dtype=F8),
         de=vm(e, L, dtype=BF),
         dg=vm(own, L, dtype=BF),
+        dy=vm(e, L, dtype=BF),
+        ndy=vm(n, L, dtype=BF),
+        ndz=vm(n, L, dtype=BF),
+        part=vm(tab, L, dtype=BF),
+        other=vm(n, L, dtype=BF),
         acc=vm(n, L),
         layers=[layer(), layer()],
     )
@@ -164,6 +169,9 @@
         live=vm(NC, L),
         acc_b=vm(L, L),
         acc_e=vm(L, L),
+        block_s=vm(EF, L, dtype=I16),
+        block_r=vm(EF, L, dtype=I16),
+        delta=vm(2 * BLOCKS + HALO, L),
         halo_col=vm(HALO, L, dtype=I16),
         halo_row=vm(HALO // L, 16, L, dtype=I16),
         grad_two=vm(NF, L, dtype=BF),
@@ -261,11 +269,14 @@
 
         lax.fori_loop(1, N_COARSE, one, 0)
 
-    def spread(src, columns, rows, count):
+    def spread(src, columns, rows, count, blocks=None, shift=0):
         def one(j, carry):
             wide = jnp.broadcast_to(src[pl.ds(j, 1), :], (L, L))
             rows[j] = wide[:16, :].astype(I16)
-            columns[chunk(j, L), :] = wide.T.astype(I16)
+            tall = wide.T
+            columns[chunk(j, L), :] = tall.astype(I16)
+            if blocks is not None:
+                blocks[chunk(j, L), :] = jnp.where(tall < NF, (tall >> 4) + shift, -1).astype(I16)
             return carry
 
         lax.fori_loop(0, count, one, 0)
@@ -427,21 +438,50 @@
         into = v.S.proj if v.masked else v.S.wide
         into[v.n : v.tab, :] = dot(rest, v.W.ei[l, 128:256, :]).astype(into.dtype)
 
+    def edge_base():
+        S, w, h = R.f, I.fw.ei, R.state_one[...]
+        S.wide[0:NF, :] = dot(h, w[1, 128:256, :])
+        S.wide[NF : 2 * NF, :] = dot(h, w[1, 256:384, :])
+        values = S.wide[0 : 2 * NF, :]
+        scale = scale_for(column_peak(values))
+        S.proj8[0 : 2 * NF, :] = halves(values, scale)
+
+        def one(i, carry):
+            rows = chunk(i, fine.tile)
+            columns = ((S.cs[rows, :], 0, 0, NF), (S.cr[rows, :], 0, NF, NF))
+            z = joined(gather_rows(columns, S.proj8), scale) + dot(S.layers[0].e[rows, :], w[1, 0:128, :])
+            S.layers[1].slope[rows, :] = z
+            return carry
+
+        lax.fori_loop(0, EF // fine.tile, one, 0)
+
+    def edge_delta(rows):
+        S = R.f
+        lanes = iota((16, L), 1).astype(I16)
+        lanes = jnp.concatenate([lanes] * (fine.tile // 16), axis=0)
+        hot = ones_where((R.block_s[rows, :] == lanes) | (R.block_r[rows, :] == lanes)).astype(F8)
+        return dot(hot, S.proj8[0 : 2 * BLOCKS, :]) + gather_rows(((S.cs[rows, :], NF, 2 * BLOCKS, HALO),), S.proj8)
+
     def forward(v, l, edges):
         S, W, A = v.S, v.W, v.S.layers[l]
-        if not v.masked:
+        based = l == 1 and not v.masked
+        if based:
+            scale = scale_for(column_peak(R.delta[...]))
+            S.proj8[0 : 2 * BLOCKS + HALO, :] = halves(R.delta[...], scale)
+        elif not v.masked:
             scale = scale_for(column_peak(S.wide[...]))
             S.proj8[...] = halves(S.wide[...], scale)
 
         def one(i, peak):
             rows = chunk(i, v.tile)
             old = edges[rows, :]
-            columns = ((S.cs[rows, :], 0, v.tab), (S.cr[rows, :], v.tab, v.own))
-            if v.masked:
-                z = gather_rows(columns, S.proj)
+            columns = ((S.cs[rows, :], 0, 0, v.tab), (S.cr[rows, :], 0, v.tab, v.own))
+            if based:
+                z = A.slope[rows, :] + joined(edge_delta(rows), scale)
+            elif v.masked:
+                z = gather_rows(columns, S.proj) + dot(old, W.ei[l, 0:128, :])
             else:
-                z = joined(gather_rows(columns, S.proj8), scale)
-            z = z + dot(old, W.ei[l, 0:128, :])
+                z = joined(gather_rows(columns, S.proj8), scale) + dot(old, W.ei[l, 0:128, :])
             gate = jax.nn.sigmoid(z)
             hidden = z * gate
             A.slope[rows, :] = gate * (1.0 + z - hidden)
@@ -490,7 +530,7 @@
             new = new * R.live[...]
         return new.astype(BF)
 
-    def backward(v, l, edges, grad, edge_grad, send_rest, keep_edge, edges_done):
+    def backward(v, l, edges, grad, edge_grad, send_rest, keep_edge, edges_done, parts_done):
         S, W, A = v.S, v.W, v.S.layers[l]
         s, acc, gw = v.first + l, v.S.acc, R.gw
         dn = grad.astype(F32)
@@ -498,7 +538,8 @@
             dn = dn * R.live[...]
         dy = normed_back(dn, A.n2[...], A.scale2[...]).astype(BF)
         dz = (dot_nt(dy, W.no[l]) * A.slope2[...]).astype(BF)
-        h = A.tab[0 : v.n, :]
+        S.ndy[...] = dy
+        S.ndz[...] = dz
         dg = dot_nt(dz, W.ni[l, 128:256, :])
         if v.masked:
             S.dg[0 : v.n, :] = dg.astype(BF)
@@ -506,15 +547,10 @@
             dg_scale = scale_for(column_peak(dg))
             S.dg8[...] = halves(dg, dg_scale)
         acc[...] = dn + dot_nt(dz, W.ni[l, 0:128, :])
-        gw[s, 512:640, :] = dot_tn(h, dz).astype(BF)
-        gw[s, 640:768, :] = dot_tn(A.g[...], dz).astype(BF)
-        gw[s, 768:896, :] = dot_tn(A.hid2[...], dy).astype(BF)
-        R.acc_b[...] = jnp.zeros((L, L), F32)
-        R.acc_e[...] = jnp.zeros((L, L), F32)
 
         def one(i, peak):
             rows = chunk(i, v.tile)
-            columns = ((S.cr[rows, :], 0, v.own),)
+            columns = ((S.cr[rows, :], 0, 0, v.own),)
             if v.masked:
                 dn = gather_rows(columns, S.dg)
             else:
@@ -523,14 +559,39 @@
                 dn = dn + edge_grad[rows, :].astype(F32)
             dy = normed_back(dn, A.n[rows, :], A.scale[rows, :]).astype(BF)
             dz = (dot_nt(dy, W.eo[l]) * A.slope[rows, :]).astype(BF)
+            S.dy[rows, :] = dy
             S.dz[rows, :] = dz
-            R.acc_b[...] += dot_tn(A.hid[rows, :], dy)
-            R.acc_e[...] += dot_tn(edges[rows, :], dz)
             if keep_edge:
-                S.de[rows, :] = (dn + dot_nt(dz, W.ei[l, 0:128, :])).astype(BF)
+                S.de[rows, :] = dn.astype(BF)
             return jnp.maximum(peak, column_peak(dz.astype(F32)))
 
         peak = lax.fori_loop(0, v.e // v.tile, one, jnp.zeros((1, L), F32))
+
+        def edge_weights():
+            gw[s, 512:640, :] = dot_tn(A.tab[0 : v.n, :], S.ndz[...]).astype(BF)
+            gw[s, 640:768, :] = dot_tn(A.g[...], S.ndz[...]).astype(BF)
+            gw[s, 768:896, :] = dot_tn(A.hid2[...], S.ndy[...]).astype(BF)
+            R.acc_b[...] = jnp.zeros((L, L), F32)
+            R.acc_e[...] = jnp.zeros((L, L), F32)
+
+            def add(i, carry):
+                rows = chunk(i, v.tile)
+                dz = S.dz[rows, :]
+                R.acc_b[...] += dot_tn(A.hid[rows, :], S.dy[rows, :])
+                R.acc_e[...] += dot_tn(edges[rows, :], dz)
+                if keep_edge:
+                    S.de[rows, :] = (S.de[rows, :].astype(F32) + dot_nt(dz, W.ei[l, 0:128, :])).astype(BF)
+                return carry
+
+            lax.fori_loop(0, v.e // v.tile, add, 0)
+            gw[s, 256:384, :] = R.acc_e[...].astype(BF)
+            gw[s, 384:512, :] = R.acc_b[...].astype(BF)
+
+        def node_weights():
+            gw[s, 0:128, :] = dot_tn(A.tab[0 : v.used, :], S.part[0 : v.used, :]).astype(BF)
+            gw[s, 128:256, :] = dot_tn(A.tab[0 : v.n, :], S.other[...]).astype(BF)
+
+        edges_done(edge_weights)
         if v.masked:
 
             def spread_back(rows_ref, first, count):
@@ -549,27 +610,20 @@
             def spread_back(rows_ref, first, count):
                 return joined(scatter_rows(rows_ref, S.e8, first, count, v.e), scale).astype(BF)
 
-        gw[s, 256:384, :] = R.acc_e[...].astype(BF)
-        gw[s, 384:512, :] = R.acc_b[...].astype(BF)
-        edges_done()
         rest = spread_back(S.rs, v.n, v.used - v.n)
+        S.part[v.n : v.used, :] = rest
         send_rest(dot_nt(rest, W.ei[l, 128:256, :]).astype(BF))
-        R.acc_b[...] = dot_tn(A.tab[v.n : v.used, :], rest)
-        R.acc_e[...] = jnp.zeros((L, L), F32)
 
         def two(i, carry):
             rows = chunk(i, v.block)
-            h = A.tab[rows, :]
-            part = spread_back(S.rs, i * v.block, v.block)
-            R.acc_b[...] += dot_tn(h, part)
-            other = spread_back(S.rr, i * v.block, v.block)
-            R.acc_e[...] += dot_tn(h, other)
-            acc[rows, :] += dot_nt(part, W.ei[l, 128:256, :]) + dot_nt(other, W.ei[l, 256:384, :])
+            S.part[rows, :] = spread_back(S.rs, i * v.block, v.block)
+            S.other[rows, :] = spread_back(S.rr, i * v.block, v.block)
             return carry
 
         lax.fori_loop(0, v.n // v.block, two, 0)
-        gw[s, 0:128, :] = R.acc_b[...].astype(BF)
-        gw[s, 128:256, :] = R.acc_e[...].astype(BF)
+        parts_done(node_weights)
+        acc[...] += dot_nt(S.part[0 : v.n, :], W.ei[l, 128:256, :]) + dot_nt(S.other[...], W.ei[l, 256:384, :])
+        return edge_weights, node_weights
 
     def place_column():
         return R.place[0][...]
@@ -648,7 +702,7 @@
         return jnp.broadcast_to(lane_sum(jnp.where(iota((NC, L), 1) == within, row, 0.0)), (NC, L))
 
     def halo_pick(tab, k):
-        R.hs[k][...] = gather_rows(((R.halo_col[...], 0, NF),), tab).astype(BF)
+        R.hs[k][...] = gather_rows(((R.halo_col[...], 0, 0, NF),), tab).astype(BF)
 
     def halo_back(k):
         def send(values):
@@ -686,15 +740,17 @@
         for copy in copies:
             copy.wait()
 
-    def nothing():
+    later = []
+
+    def nothing(run):
         pass
 
     def enter():
         greet()
         spread(I.halo, R.halo_col, R.halo_row, HALO // L)
         halo_pick(I.node, 0)
-        spread(I.src, R.f.cs, R.f.rs, EF // L)
-        spread(I.dst, R.f.cr, R.f.rr, EF // L)
+        spread(I.src, R.f.cs, R.f.rs, EF // L, R.block_s)
+        spread(I.dst, R.f.cr, R.f.rr, EF // L, R.block_r, BLOCKS)
         pl.semaphore_wait(barrier, N_FINE - 1 + N_COARSE - 1)
         halo_start(R.hs[0], R.f.layers[0].tab, NF, R.hs_sem[0])
 
@@ -707,7 +763,7 @@
         R.parts[3 * NC : 512, :] = jnp.zeros((512 - 3 * NC, L), BF)
         R.c.proj[512 + NC : 768, :] = jnp.zeros((256 - NC, L), BF)
         R.c.dg[NC:256, :] = jnp.zeros((256 - NC, L), BF)
-        owner = jnp.broadcast_to(I.owner[...], (BLOCKS, L))
+        owner = jnp.broadcast_to(I.owner[...], (L, BLOCKS)).T
         below = jnp.full((L - BLOCKS, L), -1, I32)
         square = jnp.concatenate([owner, below], axis=0).T
         same = (owner == square[0:BLOCKS, :]) & (iota((BLOCKS, L), 1) < iota((BLOCKS, L), 0))
@@ -725,6 +781,7 @@
         pooled = (dot(pool_hot(), R.state_one[...]) * (1.0 / POOL)).astype(BF)
         R.ws[0][...] = (dot(put_three(), pooled) + put_flags()).astype(BF)
         wide_start(0)
+        edge_base()
         wide_wait(0)
         arrived = R.wr[0][...]
         R.c.layers[0].tab[...] = dot(across_hot(512, three_of), arrived).astype(BF)
@@ -753,15 +810,19 @@
         R.f.layers[1].tab[0:NF, :] = (R.state_one[...].astype(F32) + dot(grow_hot(), picked)).astype(BF)
         halo_pick(R.f.layers[1].tab, 1)
         halo_start(R.hs[1], R.f.layers[1].tab, NF, R.hs_sem[1])
-        project_own(fine, 1)
+        w = I.fw.ei
+        R.delta[0:BLOCKS, :] = dot(picked, w[1, 128:256, :])
+        R.delta[BLOCKS : 2 * BLOCKS, :] = dot(picked, w[1, 256:384, :])
         halo_wait(R.hs[1], R.f.layers[1].tab, NF, R.hs_sem[1])
-        project_rest(fine, 1)
+        R.delta[2 * BLOCKS :, :] = dot(R.f.layers[1].tab[NF : NF + HALO, :], w[1, 128:256, :])
 
     def fine_one():
         O.new_state[...] = forward(fine, 1, R.f.layers[0].e)
 
     def fine_one_back():
-        backward(fine, 1, R.f.layers[0].e, I.cot[...], None, halo_back(2), True, nothing)
+        later[:] = backward(
+            fine, 1, R.f.layers[0].e, I.cot[...], None, halo_back(2), True, nothing, nothing
+        )
 
     def sink_back():
         halo_add(2)
@@ -769,6 +830,8 @@
         R.grad_two[...] = grad_two
         R.ws[2][...] = dot(put_hot(), dot(pool_hot(), grad_two).astype(BF)).astype(BF)
         wide_start(2)
+        for run in later:
+            run()
         total[1].one()
         wide_wait(2)
         R.grad_c[...] = dot(across_hot(NC, slot_of), R.wr[2][...]).astype(BF)
@@ -783,17 +846,23 @@
                     R.parts[NC : 3 * NC, :] = values
 
             edges, edge_grad = (I.cedge, R.c.de) if l == 0 else (R.c.layers[0].e, None)
-            backward(coarse, l, edges, R.grad_c[...], edge_grad, send, l == 1, nothing)
+            weights = backward(
+                coarse, l, edges, R.grad_c[...], edge_grad, send, l == 1, nothing, nothing
+            )
             if l == 1:
+                for run in weights:
+                    run()
                 total[3].one()
+                wait(near_grad())
                 total[1].two()
-                wait(near_grad())
                 grad = R.c.acc[...] + R.nr[0:NC, :].astype(F32) + R.nr[NC : 2 * NC, :].astype(F32)
                 R.grad_c[...] = grad.astype(BF)
             else:
                 R.parts[0:NC, :] = R.c.acc[...].astype(BF)
                 R.ws[3][...] = dot(apart_hot(three_of, 512), R.parts[...]).astype(BF)
                 wide_start(3)
+                for run in weights:
+                    run()
 
         return run
 
@@ -806,14 +875,18 @@
         R.grad_one[...] = (R.grad_two[...].astype(F32) + dot(grow_hot(), sunk)).astype(BF)
 
     def fine_zero_back():
-        def edges_done():
+        def edges_done(edge_weights):
+            edge_weights()
             total[0].one()
             total[2].two()
             total[3].three()
 
-        backward(fine, 0, I.edge, R.grad_one[...], R.f.de, halo_back(3), False, edges_done)
-        R.late[...] = R.gw[0, 0:LATE, :].astype(F32)
-        late.one()
+        def parts_done(node_weights):
+            node_weights()
+            R.late[...] = R.gw[0, 0:LATE, :].astype(F32)
+            late.one()
+
+        backward(fine, 0, I.edge, R.grad_one[...], R.f.de, halo_back(3), False, edges_done, parts_done)
 
     def leave():
         total[0].two()
@@ -859,6 +932,7 @@
     arrays = list(arrays)
     for i, rows in ((3, EF // L), (4, EF // L), (7, EC // L), (8, EC // L)):
         arrays[i] = arrays[i].reshape(rows, L)
+    arrays[6] = arrays[6].reshape(1, BLOCKS)
     states = [jax.ShapeDtypeStruct((NF, L), BF)] * 2
     vm_spec = pl.BlockSpec(memory_space=pltpu.VMEM)
     any_spec = pl.BlockSpec(memory_space=pl.ANY)

time: 141 us -> 132 us (0.936)
  Pallas kernels: 138 us -> 130 us
    pallas_call x1, Pallas kernels: 135 us -> 127 us  [body(): pl.pallas_call(kernel, out_shape=tuple(states + [jax.ShapeDtypeStruct((4,...]
where the time goes in v3:
time: 132 us; the launch traced here: 131 us
  Pallas kernels  130 us (98%)
    pallas_call x1, Pallas kernels, body(): pl.pallas_call(kernel, out_shape=tuple(states + [jax.ShapeDtypeStruct((4,...  127 us
    pallas_call x1, Pallas kernels, body(): pl.pallas_call(spread_out, out_shape=tuple(outs), in_specs=[vm_spec] * 3,...  3.25 us

profile of v3, /device:TPU:1, one launch (start us, length us, event | category | flops | bytes accessed | tf_op | source)
XLA Modules:
  0.0 131.1 jit_solution(12038732491938485591)
XLA Ops:
  0.7 127.0 %shard_map.249 = (bf16[1024,128]{1,0:T(8,128)(2,1)}, bf16[1024,128]{1,0:T(8,128)(2,1)}, f32[4,896,128]{2,1,0:T(8,128)}) custom-call(bf16[1024,128]{1,0:T(8,128)(2,1)} %args_0_.4, bf16[4096,128]{1,0:T(8,128)(2,1)} %args_1_.4, bf16[640,128]{1,0:T(8,128)(2,1)} %args_2_.4, s32[32,128]{1,0:T(8,128)} %bitcast.5, s32[32,128]{1,0:T(8,128)} %bitcast.6, ...), custom_call_target="tpu_custom_call" | custom-call | flops 40000000000 | bytes 8388608 | tf_op jit(solution)/shard_map/pallas_call | solution.py:939
  127.6 3.2 %shard_map.250 = (bf16[1024,128]{1,0:T(8,128)(2,1)}, bf16[1024,128]{1,0:T(8,128)(2,1)}, f32[2,384,128]{2,1,0:T(8,128)}, f32[2,128,128]{2,1,0:T(8,128)}, f32[2,25...) custom-call(bf16[1024,128]{1,0:T(8,128)(2,1)} %get-tuple-element.13., ...), custom_call_target="tpu_custom_call" | custom-call | tf_op jit(solution)/shard_map/pallas_call | solution.py:953

commit v4 on v3

--- a/solution.py
+++ b/solution.py
@@ -143,7 +143,7 @@
         rs=vm(e // L, 16, L, dtype=I16),
         rr=vm(e // L, 16, L, dtype=I16),
         proj=vm(tab + own, L, dtype=BF),
-        wide=vm(tab + own, L),
+        wide=vm(2 * n, L),
         proj8=vm(tab + own, 2 * L, dtype=F8),
         dz=vm(e, L, dtype=BF),
         e8=vm(e, 2 * L, dtype=F8),
@@ -279,7 +279,7 @@
                 blocks[chunk(j, L), :] = jnp.where(tall < NF, (tall >> 4) + shift, -1).astype(I16)
             return carry
 
-        lax.fori_loop(0, count, one, 0)
+        lax.fori_loop(0, count, one, 0, unroll=next(u for u in (8, 5, 4) if count % u == 0))
 
     def halo_copies(src, dst, base, sem):
         out, back = [], []
@@ -429,19 +429,17 @@
 
     def project_own(v, l):
         w, h = v.W.ei, v.S.layers[l].tab[0 : v.n, :]
-        into = v.S.proj if v.masked else v.S.wide
-        into[0 : v.n, :] = dot(h, w[l, 128:256, :]).astype(into.dtype)
-        into[v.tab : v.tab + v.n, :] = dot(h, w[l, 256:384, :]).astype(into.dtype)
+        v.S.proj[0 : v.n, :] = dot(h, w[l, 128:256, :]).astype(BF)
+        v.S.proj[v.tab : v.tab + v.n, :] = dot(h, w[l, 256:384, :]).astype(BF)
 
     def project_rest(v, l):
         rest = v.S.layers[l].tab[v.n : v.tab, :]
-        into = v.S.proj if v.masked else v.S.wide
-        into[v.n : v.tab, :] = dot(rest, v.W.ei[l, 128:256, :]).astype(into.dtype)
-
-    def edge_base():
-        S, w, h = R.f, I.fw.ei, R.state_one[...]
-        S.wide[0:NF, :] = dot(h, w[1, 128:256, :])
-        S.wide[NF : 2 * NF, :] = dot(h, w[1, 256:384, :])
+        v.S.proj[v.n : v.tab, :] = dot(rest, v.W.ei[l, 128:256, :]).astype(BF)
+
+    def edge_base(l, h, edges):
+        S, w = R.f, I.fw.ei
+        S.wide[0:NF, :] = dot(h, w[l, 128:256, :])
+        S.wide[NF : 2 * NF, :] = dot(h, w[l, 256:384, :])
         values = S.wide[0 : 2 * NF, :]
         scale = scale_for(column_peak(values))
         S.proj8[0 : 2 * NF, :] = halves(values, scale)
@@ -449,39 +447,36 @@
         def one(i, carry):
             rows = chunk(i, fine.tile)
             columns = ((S.cs[rows, :], 0, 0, NF), (S.cr[rows, :], 0, NF, NF))
-            z = joined(gather_rows(columns, S.proj8), scale) + dot(S.layers[0].e[rows, :], w[1, 0:128, :])
-            S.layers[1].slope[rows, :] = z
+            z = joined(gather_rows(columns, S.proj8), scale) + dot(edges[rows, :], w[l, 0:128, :])
+            S.layers[l].slope[rows, :] = z
             return carry
 
         lax.fori_loop(0, EF // fine.tile, one, 0)
 
-    def edge_delta(rows):
+    def edge_delta(l, rows):
         S = R.f
+        received = gather_rows(((S.cs[rows, :], NF, 2 * BLOCKS, HALO),), S.proj8)
+        if l == 0:
+            return received
         lanes = iota((16, L), 1).astype(I16)
         lanes = jnp.concatenate([lanes] * (fine.tile // 16), axis=0)
         hot = ones_where((R.block_s[rows, :] == lanes) | (R.block_r[rows, :] == lanes)).astype(F8)
-        return dot(hot, S.proj8[0 : 2 * BLOCKS, :]) + gather_rows(((S.cs[rows, :], NF, 2 * BLOCKS, HALO),), S.proj8)
+        return dot(hot, S.proj8[0 : 2 * BLOCKS, :]) + received
 
     def forward(v, l, edges):
         S, W, A = v.S, v.W, v.S.layers[l]
-        based = l == 1 and not v.masked
-        if based:
+        if not v.masked:
             scale = scale_for(column_peak(R.delta[...]))
             S.proj8[0 : 2 * BLOCKS + HALO, :] = halves(R.delta[...], scale)
-        elif not v.masked:
-            scale = scale_for(column_peak(S.wide[...]))
-            S.proj8[...] = halves(S.wide[...], scale)
 
         def one(i, peak):
             rows = chunk(i, v.tile)
             old = edges[rows, :]
-            columns = ((S.cs[rows, :], 0, 0, v.tab), (S.cr[rows, :], 0, v.tab, v.own))
-            if based:
-                z = A.slope[rows, :] + joined(edge_delta(rows), scale)
-            elif v.masked:
+            if v.masked:
+                columns = ((S.cs[rows, :], 0, 0, v.tab), (S.cr[rows, :], 0, v.tab, v.own))
                 z = gather_rows(columns, S.proj) + dot(old, W.ei[l, 0:128, :])
             else:
-                z = joined(gather_rows(columns, S.proj8), scale) + dot(old, W.ei[l, 0:128, :])
+                z = A.slope[rows, :] + joined(edge_delta(l, rows), scale)
             gate = jax.nn.sigmoid(z)
             hidden = z * gate
             A.slope[rows, :] = gate * (1.0 + z - hidden)
@@ -751,18 +746,19 @@
         halo_pick(I.node, 0)
         spread(I.src, R.f.cs, R.f.rs, EF // L, R.block_s)
         spread(I.dst, R.f.cr, R.f.rr, EF // L, R.block_r, BLOCKS)
+        edge_base(0, I.node[...], I.edge)
         pl.semaphore_wait(barrier, N_FINE - 1 + N_COARSE - 1)
         halo_start(R.hs[0], R.f.layers[0].tab, NF, R.hs_sem[0])
 
     def prepare():
         R.f.layers[0].tab[0:NF, :] = I.node[...]
-        project_own(fine, 0)
         spread(I.csrc, R.c.cs, R.c.rs, EC // L)
         spread(I.cdst, R.c.cr, R.c.rr, EC // L)
         R.c.layers[1].tab[3 * NC : 512, :] = jnp.zeros((512 - 3 * NC, L), BF)
         R.parts[3 * NC : 512, :] = jnp.zeros((512 - 3 * NC, L), BF)
         R.c.proj[512 + NC : 768, :] = jnp.zeros((256 - NC, L), BF)
         R.c.dg[NC:256, :] = jnp.zeros((256 - NC, L), BF)
+        R.delta[0 : 2 * BLOCKS, :] = jnp.zeros((2 * BLOCKS, L), F32)
         owner = jnp.broadcast_to(I.owner[...], (L, BLOCKS)).T
         below = jnp.full((L - BLOCKS, L), -1, I32)
         square = jnp.concatenate([owner, below], axis=0).T
@@ -772,16 +768,20 @@
         R.place[0][...] = place
         R.place[1][...] = jnp.concatenate([place, below], axis=0).T
 
+    def received(l):
+        rows = R.f.layers[l].tab[NF : NF + HALO, :]
+        R.delta[2 * BLOCKS :, :] = dot(rows, I.fw.ei[l, 128:256, :])
+
     def fine_zero():
         halo_wait(R.hs[0], R.f.layers[0].tab, NF, R.hs_sem[0])
-        project_rest(fine, 0)
+        received(0)
         R.state_one[...] = forward(fine, 0, I.edge)
 
     def sink():
         pooled = (dot(pool_hot(), R.state_one[...]) * (1.0 / POOL)).astype(BF)
         R.ws[0][...] = (dot(put_three(), pooled) + put_flags()).astype(BF)
         wide_start(0)
-        edge_base()
+        edge_base(1, R.state_one[...], R.f.layers[0].e)
         wide_wait(0)
         arrived = R.wr[0][...]
         R.c.layers[0].tab[...] = dot(across_hot(512, three_of), arrived).astype(BF)
@@ -814,7 +814,7 @@
         R.delta[0:BLOCKS, :] = dot(picked, w[1, 128:256, :])
         R.delta[BLOCKS : 2 * BLOCKS, :] = dot(picked, w[1, 256:384, :])
         halo_wait(R.hs[1], R.f.layers[1].tab, NF, R.hs_sem[1])
-        R.delta[2 * BLOCKS :, :] = dot(R.f.layers[1].tab[NF : NF + HALO, :], w[1, 128:256, :])
+        received(1)
 
     def fine_one():
         O.new_state[...] = forward(fine, 1, R.f.layers[0].e)

time: 132 us -> 128 us (0.970)
  Pallas kernels: 130 us -> 125 us
    pallas_call x1, Pallas kernels: 127 us -> 122 us  [body(): pl.pallas_call(kernel, out_shape=tuple(states + [jax.ShapeDtypeStruct((4,...]
where the time goes in v4:
time: 128 us; the launch traced here: 126 us
  Pallas kernels  125 us (98%)
    pallas_call x1, Pallas kernels, body(): pl.pallas_call(kernel, out_shape=tuple(states + [jax.ShapeDtypeStruct((4,...  122 us
    pallas_call x1, Pallas kernels, body(): pl.pallas_call(spread_out, out_shape=tuple(outs), in_specs=[vm_spec] * 3,...  3.25 us

profile of v4, /device:TPU:1, one launch (start us, length us, event | category | flops | bytes accessed | tf_op | source)
XLA Modules:
  0.0 126.0 jit_solution(7854867755593523356)
XLA Ops:
  0.7 121.9 %shard_map.249 = (bf16[1024,128]{1,0:T(8,128)(2,1)}, bf16[1024,128]{1,0:T(8,128)(2,1)}, f32[4,896,128]{2,1,0:T(8,128)}) custom-call(bf16[1024,128]{1,0:T(8,128)(2,1)} %args_0_.4, bf16[4096,128]{1,0:T(8,128)(2,1)} %args_1_.4, bf16[640,128]{1,0:T(8,128)(2,1)} %args_2_.4, s32[32,128]{1,0:T(8,128)} %bitcast.5, s32[32,128]{1,0:T(8,128)} %bitcast.6, ...), custom_call_target="tpu_custom_call" | custom-call | flops 40000000000 | bytes 8388608 | tf_op jit(solution)/shard_map/pallas_call | solution.py:939
  122.5 3.2 %shard_map.250 = (bf16[1024,128]{1,0:T(8,128)(2,1)}, bf16[1024,128]{1,0:T(8,128)(2,1)}, f32[2,384,128]{2,1,0:T(8,128)}, f32[2,128,128]{2,1,0:T(8,128)}, f32[2,25...) custom-call(bf16[1024,128]{1,0:T(8,128)(2,1)} %get-tuple-element.13., ...), custom_call_target="tpu_custom_call" | custom-call | tf_op jit(solution)/shard_map/pallas_call | solution.py:953

commit v5 on v4

--- a/solution.py
+++ b/solution.py
@@ -172,6 +172,21 @@
         block_s=vm(EF, L, dtype=I16),
         block_r=vm(EF, L, dtype=I16),
         delta=vm(2 * BLOCKS + HALO, L),
+        hot=SimpleNamespace(
+            pool=vm(BLOCKS, NF, dtype=BF),
+            grow=vm(NF, BLOCKS, dtype=BF),
+            three=vm(WIDE, BLOCKS, dtype=BF),
+            flags=vm(WIDE, L),
+            put=vm(WIDE, BLOCKS, dtype=BF),
+            take=vm(BLOCKS, WIDE, dtype=BF),
+            take_three=vm(BLOCKS, WIDE, dtype=BF),
+            across=vm(512, WIDE, dtype=BF),
+            narrow=vm(NC, WIDE, dtype=BF),
+            widen=vm(WIDE, 256, dtype=BF),
+            apart=vm(WIDE, 512, dtype=BF),
+            flag_row=vm(NC, WIDE, dtype=BF),
+            flag_lane=vm(NC, L),
+        ),
         halo_col=vm(HALO, L, dtype=I16),
         halo_row=vm(HALO // L, 16, L, dtype=I16),
         grad_two=vm(NF, L, dtype=BF),
@@ -267,7 +282,8 @@
             pl.semaphore_signal(barrier, inc=1, device_id=(f, coarse_at(d)), device_id_type=MESH)
             return carry
 
-        lax.fori_loop(1, N_COARSE, one, 0)
+        lax.fori_loop(N_COARSE // 2, N_COARSE, one, 0)
+        lax.fori_loop(1, N_COARSE // 2, one, 0)
 
     def spread(src, columns, rows, count, blocks=None, shift=0):
         def one(j, carry):
@@ -687,14 +703,29 @@
             parts.append(ones_where(at == here))
         return jnp.concatenate(parts, axis=1)
 
-    def live_rows(arrived):
+    def flag_places():
         slot = iota((NC, WIDE), 0)
         first = (iota((NC, WIDE), 1) >> 4) * CAP
         last_row = (iota((NC, WIDE), 1) & (PAD - 1)) == PAD - 1
-        row = dot(ones_where(last_row & (slot >= first) & (slot < first + CAP)), arrived)
+        row = ones_where(last_row & (slot >= first) & (slot < first + CAP))
         count = iota((NC, L), 0).astype(F32)
         within = iota((NC, L), 0) - jnp.floor((count + 0.5) * (1.0 / CAP)).astype(I32) * CAP
-        return jnp.broadcast_to(lane_sum(jnp.where(iota((NC, L), 1) == within, row, 0.0)), (NC, L))
+        return row, jnp.where(iota((NC, L), 1) == within, 1.0, 0.0)
+
+    def build_hot():
+        hot = R.hot
+        hot.pool[...] = pool_hot()
+        hot.grow[...] = grow_hot()
+        hot.three[...] = put_three()
+        hot.flags[...] = put_flags()
+        hot.put[...] = put_hot()
+        hot.take[...] = take_hot()
+        hot.take_three[...] = take_three()
+        hot.across[...] = across_hot(512, three_of)
+        hot.narrow[...] = across_hot(NC, slot_of)
+        hot.widen[...] = apart_hot(slot_of, 256)
+        hot.apart[...] = apart_hot(three_of, 512)
+        hot.flag_row[...], hot.flag_lane[...] = flag_places()
 
     def halo_pick(tab, k):
         R.hs[k][...] = gather_rows(((R.halo_col[...], 0, 0, NF),), tab).astype(BF)
@@ -767,6 +798,7 @@
         place = owner * PAD + rank
         R.place[0][...] = place
         R.place[1][...] = jnp.concatenate([place, below], axis=0).T
+        build_hot()
 
     def received(l):
         rows = R.f.layers[l].tab[NF : NF + HALO, :]
@@ -778,14 +810,15 @@
         R.state_one[...] = forward(fine, 0, I.edge)
 
     def sink():
-        pooled = (dot(pool_hot(), R.state_one[...]) * (1.0 / POOL)).astype(BF)
-        R.ws[0][...] = (dot(put_three(), pooled) + put_flags()).astype(BF)
+        pooled = (dot(R.hot.pool[...], R.state_one[...]) * (1.0 / POOL)).astype(BF)
+        R.ws[0][...] = (dot(R.hot.three[...], pooled) + R.hot.flags[...]).astype(BF)
         wide_start(0)
         edge_base(1, R.state_one[...], R.f.layers[0].e)
         wide_wait(0)
         arrived = R.wr[0][...]
-        R.c.layers[0].tab[...] = dot(across_hot(512, three_of), arrived).astype(BF)
-        R.live[...] = live_rows(arrived)
+        R.c.layers[0].tab[...] = dot(R.hot.across[...], arrived).astype(BF)
+        row = dot(R.hot.flag_row[...], arrived) * R.hot.flag_lane[...]
+        R.live[...] = jnp.broadcast_to(lane_sum(row), (NC, L))
 
     def coarse_layer(l):
         def run():
@@ -799,15 +832,15 @@
             if l == 0:
                 R.c.layers[1].tab[0:NC, :] = new
             else:
-                R.ws[1][...] = dot(apart_hot(slot_of, 256)[:, 0:NC], new).astype(BF)
+                R.ws[1][...] = dot(R.hot.widen[:, 0:NC], new).astype(BF)
                 wide_start(1)
 
         return run
 
     def rise():
         wide_wait(1)
-        picked = dot(take_hot(), R.wr[1][...]).astype(BF)
-        R.f.layers[1].tab[0:NF, :] = (R.state_one[...].astype(F32) + dot(grow_hot(), picked)).astype(BF)
+        picked = dot(R.hot.take[...], R.wr[1][...]).astype(BF)
+        R.f.layers[1].tab[0:NF, :] = (R.state_one[...].astype(F32) + dot(R.hot.grow[...], picked)).astype(BF)
         halo_pick(R.f.layers[1].tab, 1)
         halo_start(R.hs[1], R.f.layers[1].tab, NF, R.hs_sem[1])
         w = I.fw.ei
@@ -828,13 +861,13 @@
         halo_add(2)
         grad_two = R.f.acc[...].astype(BF)
         R.grad_two[...] = grad_two
-        R.ws[2][...] = dot(put_hot(), dot(pool_hot(), grad_two).astype(BF)).astype(BF)
+        R.ws[2][...] = dot(R.hot.put[...], dot(R.hot.pool[...], grad_two).astype(BF)).astype(BF)
         wide_start(2)
         for run in later:
             run()
         total[1].one()
         wide_wait(2)
-        R.grad_c[...] = dot(across_hot(NC, slot_of), R.wr[2][...]).astype(BF)
+        R.grad_c[...] = dot(R.hot.narrow[...], R.wr[2][...]).astype(BF)
 
     def coarse_back(l):
         def run():
@@ -859,7 +892,7 @@
                 R.grad_c[...] = grad.astype(BF)
             else:
                 R.parts[0:NC, :] = R.c.acc[...].astype(BF)
-                R.ws[3][...] = dot(apart_hot(three_of, 512), R.parts[...]).astype(BF)
+                R.ws[3][...] = dot(R.hot.apart[...], R.parts[...]).astype(BF)
                 wide_start(3)
                 for run in weights:
                     run()
@@ -871,8 +904,8 @@
         total[1].three()
         total[3].two()
         wide_wait(3)
-        sunk = (dot(take_three(), R.wr[3][...]).astype(BF).astype(F32) * (1.0 / POOL)).astype(BF)
-        R.grad_one[...] = (R.grad_two[...].astype(F32) + dot(grow_hot(), sunk)).astype(BF)
+        sunk = (dot(R.hot.take_three[...], R.wr[3][...]).astype(BF).astype(F32) * (1.0 / POOL)).astype(BF)
+        R.grad_one[...] = (R.grad_two[...].astype(F32) + dot(R.hot.grow[...], sunk)).astype(BF)
 
     def fine_zero_back():
         def edges_done(edge_weights):
@@ -894,9 +927,9 @@
         halo_add(3)
         O.state_grad[...] = R.f.acc[...].astype(BF)
         late.two()
+        late.three()
         total[0].three()
         total[1].end()
-        late.three()
         total[3].end()
         total[2].end()
         total[0].end()

time: 128 us -> 130 us (1.016)
  the two profiles are of different devices: /device:TPU:1 before, /device:TPU:4 now
where the time goes in v5:
time: 130 us
  Pallas kernels  129 us (99%)
    pallas_call x1, Pallas kernels, body(): pl.pallas_call(kernel, out_shape=tuple(states + [jax.ShapeDtypeStruct((4,...  126 us
    pallas_call x1, Pallas kernels, body(): pl.pallas_call(spread_out, out_shape=tuple(outs), in_specs=[vm_spec] * 3,...  3.25 us

profile of v5, /device:TPU:4, one launch (start us, length us, event | category | flops | bytes accessed | tf_op | source)
XLA Modules:
  0.0 130.3 jit_solution(11494063225552563551)
XLA Ops:
  0.7 126.2 %shard_map.249 = (bf16[1024,128]{1,0:T(8,128)(2,1)}, bf16[1024,128]{1,0:T(8,128)(2,1)}, f32[4,896,128]{2,1,0:T(8,128)}) custom-call(bf16[1024,128]{1,0:T(8,128)(2,1)} %args_0_.4, bf16[4096,128]{1,0:T(8,128)(2,1)} %args_1_.4, bf16[640,128]{1,0:T(8,128)(2,1)} %args_2_.4, s32[32,128]{1,0:T(8,128)} %bitcast.5, s32[32,128]{1,0:T(8,128)} %bitcast.6, ...), custom_call_target="tpu_custom_call" | custom-call | flops 40000000000 | bytes 8388608 | tf_op jit(solution)/shard_map/pallas_call | solution.py:972
  126.8 3.2 %shard_map.250 = (bf16[1024,128]{1,0:T(8,128)(2,1)}, bf16[1024,128]{1,0:T(8,128)(2,1)}, f32[2,384,128]{2,1,0:T(8,128)}, f32[2,128,128]{2,1,0:T(8,128)}, f32[2,25...) custom-call(bf16[1024,128]{1,0:T(8,128)(2,1)} %get-tuple-element.13., ...), custom_call_target="tpu_custom_call" | custom-call | tf_op jit(solution)/shard_map/pallas_call | solution.py:986

commit v6 on v5

--- a/solution.py
+++ b/solution.py
@@ -926,10 +926,10 @@
         total[2].three()
         halo_add(3)
         O.state_grad[...] = R.f.acc[...].astype(BF)
+        total[0].three()
         late.two()
+        total[1].end()
         late.three()
-        total[0].three()
-        total[1].end()
         total[3].end()
         total[2].end()
         total[0].end()

time: 130 us -> 127 us (0.977)
  the two profiles are of different devices: /device:TPU:4 before, /device:TPU:1 now
where the time goes in v6:
time: 127 us; the launch traced here: 126 us
  Pallas kernels  125 us (98%)
    pallas_call x1, Pallas kernels, body(): pl.pallas_call(kernel, out_shape=tuple(states + [jax.ShapeDtypeStruct((4,...  122 us
    pallas_call x1, Pallas kernels, body(): pl.pallas_call(spread_out, out_shape=tuple(outs), in_specs=[vm_spec] * 3,...  3.25 us

profile of v6, /device:TPU:1, one launch (start us, length us, event | category | flops | bytes accessed | tf_op | source)
XLA Modules:
  0.0 126.1 jit_solution(4383185532490169849)
XLA Ops:
  0.7 122.0 %shard_map.249 = (bf16[1024,128]{1,0:T(8,128)(2,1)}, bf16[1024,128]{1,0:T(8,128)(2,1)}, f32[4,896,128]{2,1,0:T(8,128)}) custom-call(bf16[1024,128]{1,0:T(8,128)(2,1)} %args_0_.4, bf16[4096,128]{1,0:T(8,128)(2,1)} %args_1_.4, bf16[640,128]{1,0:T(8,128)(2,1)} %args_2_.4, s32[32,128]{1,0:T(8,128)} %bitcast.5, s32[32,128]{1,0:T(8,128)} %bitcast.6, ...), custom_call_target="tpu_custom_call" | custom-call | flops 40000000000 | bytes 8388608 | tf_op jit(solution)/shard_map/pallas_call | solution.py:972
  122.7 3.2 %shard_map.250 = (bf16[1024,128]{1,0:T(8,128)(2,1)}, bf16[1024,128]{1,0:T(8,128)(2,1)}, f32[2,384,128]{2,1,0:T(8,128)}, f32[2,128,128]{2,1,0:T(8,128)}, f32[2,25...) custom-call(bf16[1024,128]{1,0:T(8,128)(2,1)} %get-tuple-element.13., ...), custom_call_target="tpu_custom_call" | custom-call | tf_op jit(solution)/shard_map/pallas_call | solution.py:986
